TPU v7x, 128 devices: a whole 4x4x4 slice. The times are simulated.
128 devices in a mesh: dp: 8 (over x_hi, z), tensor: 16 (over x_lo, y, core).
Axes of the slice: x: 4 (x_hi: 2, x_lo: 2; x = x_hi * 2 + x_lo), y: 4, z: 4, core: 2. Of those that a mesh axis runs over, the one named last changes fastest.
Arguments:
- history: bfloat16 [17, 16384, 2048], P(None, ('dp', 'tensor')), may hold values from -6 to 6
- cotangent: bfloat16 [16384, 2048], P(('dp', 'tensor')), may hold values from -6 to 6
- lengths: int32 [8, 4], replicated, may hold values from 0 to 2048, as said below
- mix_gain: float32 [2048], replicated, may hold values from 0.5 to 1.5
- mix_first: float32 [2048, 68], replicated, may hold values from -0.125 to 0.125
- mix_second: float32 [68, 68], replicated, may hold values from -0.3 to 0.3
- mix_bias: float32 [68], replicated, may hold values from -1.8 to 1.8
- gain_query: float32 [2048], replicated, may hold values from 0.5 to 1.5
- gain_key: float32 [2048], replicated, may hold values from 0.5 to 1.5
- gain_value: float32 [2048], replicated, may hold values from 0.5 to 1.5
- gain_mlp: float32 [2048], replicated, may hold values from 0.5 to 1.5
- w_query: bfloat16 [2048, 2048], P(None, 'tensor'), may hold values from -0.125 to 0.125
- w_key: bfloat16 [2048, 2048], P(None, 'tensor'), may hold values from -0.125 to 0.125
- w_value: bfloat16 [2048, 2048], P(None, 'tensor'), may hold values from -0.125 to 0.125
- w_output: bfloat16 [2048, 2048], P('tensor'), may hold values from -1 to 1
- w_expand: bfloat16 [2048, 8192], P(None, 'tensor'), may hold values from -0.125 to 0.125
- w_reduce: bfloat16 [8192, 2048], P('tensor'), may hold values from -0.0625 to 0.0625
Outputs:
- output: bfloat16 [16384, 2048], P(('dp', 'tensor'))
- grad_history: bfloat16 [17, 16384, 2048], P(None, ('dp', 'tensor'))
- grad_mix_gain: float32 [2048], replicated
- grad_mix_first: float32 [2048, 68], replicated
- grad_mix_second: float32 [68, 68], replicated
- grad_mix_bias: float32 [68], replicated
- grad_gain_query: float32 [2048], replicated
- grad_gain_key: float32 [2048], replicated
- grad_gain_value: float32 [2048], replicated
- grad_gain_mlp: float32 [2048], replicated
- grad_w_query: float32 [2048, 2048], P('dp', 'tensor')
- grad_w_key: float32 [2048, 2048], P('dp', 'tensor')
- grad_w_value: float32 [2048, 2048], P('dp', 'tensor')
- grad_w_output: float32 [2048, 2048], P('tensor', 'dp')
- grad_w_expand: float32 [2048, 8192], P('dp', 'tensor')
- grad_w_reduce: float32 [8192, 2048], P('tensor', 'dp')
Inputs may be any that keep to these rules, and one draw needn't show every extreme that they name: Row g holds, in order, the lengths of the sequences packed into the 2048 tokens of data index g (0 marks an empty slot); each row sums to 2048, its longest entry is 1024 or more, and in some row one sequence fills all 2048 tokens.
All inputs are finite; a program needn't handle non-finite values.
Results may differ from a plain program's by a relative error of at most 0.019.
Values may be sent and summed in bfloat16 or wider, within the bound.
A program may use at most 320 MiB of HBM per device.

v0:
```python
import jax
import jax.numpy as jnp
from jax import lax
from jax.sharding import PartitionSpec as P

HEAD_DIM = 128
HISTORY = 17
STREAMS = 4
NORM_EPS = 1e-06
MASKED = -1e30
PRECISE = lax.Precision.HIGHEST


def swapped(x, axis, bit):
    return lax.ppermute(x, axis, [(i, i ^ 1 << bit) for i in range(lax.axis_size(axis))])


def rms_scale(values, gain_vector):
    inverse = lax.rsqrt(jnp.mean(values * values, axis=-1, keepdims=True) + NORM_EPS)
    return values * inverse * gain_vector


def matmul(left_side, right_side):
    return jnp.dot(left_side, right_side, precision=PRECISE)


def front_part(
    history_float, mix_gain, mix_first, mix_second, mix_bias, gain_query, gain_key, gain_value
):
    latest = rms_scale(history_float[HISTORY - 1], mix_gain)
    hidden = jax.nn.gelu(matmul(latest, mix_first), approximate=False)
    mixing = (matmul(hidden, mix_second) + mix_bias).reshape(
        history_float.shape[1], STREAMS, HISTORY
    )
    streams = jnp.einsum("tkj,jtd->ktd", mixing, history_float, precision=PRECISE)
    return (
        rms_scale(streams[0], gain_query),
        rms_scale(streams[1], gain_key),
        rms_scale(streams[2], gain_value),
        streams[3],
    )


def gelu_exact(values):
    return jax.nn.gelu(values, approximate=False)


def across_rows(left_side, right_side):
    return lax.dot_general(
        left_side, right_side, (((0,), (0,)), ((), ())), preferred_element_type=jnp.float32
    )


def across_cols(left_side, right_side):
    return lax.dot_general(
        left_side, right_side, (((1,), (1,)), ((), ())), preferred_element_type=jnp.float32
    )


def segment_of(places, doc_ends):
    return jnp.sum((places[:, None] >= doc_ends[None, :]).astype(jnp.int32), axis=1)


def gather_bits(piece, bit_list, join_dim, device_index):
    for bit_number in bit_list:
        partner = swapped(piece, "tensor", bit_number)
        upper = device_index // (1 << bit_number) % 2 == 1
        piece = jnp.where(
            upper,
            jnp.concatenate([partner, piece], axis=join_dim),
            jnp.concatenate([piece, partner], axis=join_dim),
        )
    return piece


def sum_bits(partial_value, bit_list, device_index, split_dim):
    for bit_number in reversed(bit_list):
        half_size = partial_value.shape[split_dim] // 2
        lower_half = lax.slice_in_dim(partial_value, 0, half_size, axis=split_dim)
        upper_half = lax.slice_in_dim(partial_value, half_size, 2 * half_size, axis=split_dim)
        upper = device_index // (1 << bit_number) % 2 == 1
        keep_half = jnp.where(upper, upper_half, lower_half)
        send_half = jnp.where(upper, lower_half, upper_half)
        partial_value = keep_half + swapped(
            send_half.astype(jnp.bfloat16), "tensor", bit_number
        ).astype(send_half.dtype)
    return partial_value


def make_scores(query_heads, key_heads, query_places, key_places, doc_ends):
    block_rows = min(512, query_heads.shape[0])
    scale_factor = HEAD_DIM ** (-0.5)
    query_segments = segment_of(query_places, doc_ends)
    key_segments = segment_of(key_places, doc_ends)

    def block_scores(block_index):
        scores = (
            jnp.einsum("qhd,khd->hqk", query_heads, key_heads, preferred_element_type=jnp.float32)
            * scale_factor
        )
        allowed = (query_places[:, None] >= key_places[None, :]) & (
            query_segments[:, None] == key_segments[None, :]
        )
        return (jnp.where(allowed[None], scores, MASKED), query_heads)

    return (block_scores, block_rows)


def on_device(
    history,
    cotangent,
    lengths,
    mix_gain,
    mix_first,
    mix_second,
    mix_bias,
    gain_query,
    gain_key,
    gain_value,
    gain_mlp,
    w_query,
    w_key,
    w_value,
    w_output,
    w_expand,
    w_reduce,
):
    shard_rows = history.shape[1]
    tensor_size = lax.axis_size("tensor")
    tok_group = shard_rows * tensor_size
    model_width = w_query.shape[0]
    tensor_index = lax.axis_index("tensor")
    low_bits = [0, 1]
    high_bits = list(range(2, tensor_size.bit_length() - 1))
    scale_factor = HEAD_DIM ** (-0.5)
    history_float = history.astype(jnp.float32)
    front_values, front_back = jax.vjp(
        front_part,
        history_float,
        mix_gain,
        mix_first,
        mix_second,
        mix_bias,
        gain_query,
        gain_key,
        gain_value,
    )
    query_norm, key_norm, value_norm, residual = front_values
    query_low = query_norm.astype(jnp.bfloat16)
    key_low = key_norm.astype(jnp.bfloat16)
    value_low = value_norm.astype(jnp.bfloat16)
    length_row = lax.dynamic_index_in_dim(lengths, lax.axis_index("dp"), 0, keepdims=False)
    doc_ends = jnp.cumsum(length_row)
    query_rows = gather_bits(query_low, high_bits, 0, tensor_index)
    key_rows = gather_bits(key_low, high_bits, 0, tensor_index)
    value_rows = gather_bits(value_low, high_bits, 0, tensor_index)
    cot_rows = gather_bits(cotangent, high_bits, 0, tensor_index)
    query_whole = gather_bits(w_query, low_bits, 1, tensor_index)
    key_whole = gather_bits(w_key, low_bits, 1, tensor_index)
    value_whole = gather_bits(w_value, low_bits, 1, tensor_index)
    output_whole = gather_bits(w_output, low_bits, 0, tensor_index)
    expand_whole = gather_bits(w_expand, low_bits, 1, tensor_index)
    reduce_whole = gather_bits(w_reduce, low_bits, 0, tensor_index)
    group_count = tensor_size // 4
    part_index = tensor_index % 4
    inner_rows = jnp.arange(shard_rows, dtype=jnp.int32)
    group_offsets = 4 * jnp.arange(group_count, dtype=jnp.int32)
    query_places = (
        (part_index + group_offsets)[:, None] * shard_rows + inner_rows[None, :]
    ).reshape(-1)
    key_places = (
        (jnp.arange(4, dtype=jnp.int32)[:, None, None] + group_offsets[None, :, None]) * shard_rows
        + inner_rows[None, None, :]
    ).reshape(-1)
    row_count = query_rows.shape[0]
    heads_here = query_whole.shape[1] // HEAD_DIM
    query_heads = (
        jnp.dot(query_rows, query_whole, preferred_element_type=jnp.float32)
        .astype(jnp.bfloat16)
        .reshape(row_count, heads_here, HEAD_DIM)
    )
    key_part = jnp.dot(key_rows, key_whole, preferred_element_type=jnp.float32).astype(jnp.bfloat16)
    value_part = jnp.dot(value_rows, value_whole, preferred_element_type=jnp.float32).astype(
        jnp.bfloat16
    )
    key_flat = gather_bits(key_part, low_bits, 0, tensor_index)
    value_flat = gather_bits(value_part, low_bits, 0, tensor_index)
    key_heads = key_flat.reshape(tok_group, heads_here, HEAD_DIM)
    value_heads = value_flat.reshape(tok_group, heads_here, HEAD_DIM)
    block_scores, block_rows = make_scores(
        query_heads, key_heads, query_places, key_places, doc_ends
    )
    block_count = row_count // block_rows

    def forward_block(block_index):
        masked, query_block = block_scores(block_index)
        top_score = jnp.max(masked, axis=-1, keepdims=True)
        exponent = jnp.exp(masked - top_score)
        row_total = jnp.sum(exponent, axis=-1, keepdims=True)
        weights_low = (exponent / row_total).astype(jnp.bfloat16)
        context_block = jnp.einsum(
            "hqk,khd->qhd", weights_low, value_heads, preferred_element_type=jnp.float32
        )
        return (context_block, top_score + jnp.log(row_total))

    context_blocks, log_totals = lax.map(forward_block, jnp.arange(block_count))
    context = context_blocks.reshape(row_count, heads_here * HEAD_DIM).astype(jnp.bfloat16)
    attended = sum_bits(
        jnp.dot(context, output_whole, preferred_element_type=jnp.float32),
        high_bits,
        tensor_index,
        0,
    )
    middle = residual + attended
    mlp_norm, norm_back = jax.vjp(rms_scale, middle, gain_mlp)
    mlp_low = mlp_norm.astype(jnp.bfloat16)
    mlp_gathered = gather_bits(mlp_low, high_bits, 0, tensor_index)
    expanded = jnp.dot(mlp_gathered, expand_whole, preferred_element_type=jnp.float32)
    activated, gelu_back = jax.vjp(gelu_exact, expanded)
    active_low = activated.astype(jnp.bfloat16)
    reduced = sum_bits(
        jnp.dot(active_low, reduce_whole, preferred_element_type=jnp.float32),
        high_bits,
        tensor_index,
        0,
    )
    output = (middle + reduced).astype(jnp.bfloat16)
    grad_w_reduce = across_rows(active_low, cot_rows)
    grad_active = across_cols(cot_rows, reduce_whole)
    (grad_expanded,) = gelu_back(grad_active)
    expand_low = grad_expanded.astype(jnp.bfloat16)
    grad_w_expand = across_rows(mlp_gathered, expand_low)
    grad_mlp_norm = sum_bits(across_cols(expand_low, expand_whole), high_bits, tensor_index, 0)
    grad_w_expand = sum_bits(grad_w_expand, low_bits, tensor_index, 1)
    grad_w_reduce = sum_bits(grad_w_reduce, low_bits, tensor_index, 0)
    grad_middle_norm, grad_gain_mlp = norm_back(grad_mlp_norm)
    grad_middle = cotangent.astype(jnp.float32) + grad_middle_norm
    middle_low = grad_middle.astype(jnp.bfloat16)
    middle_rows = gather_bits(middle_low, high_bits, 0, tensor_index)
    grad_w_output = across_rows(context, middle_rows)
    grad_context = (
        across_cols(middle_rows, output_whole)
        .astype(jnp.bfloat16)
        .reshape(row_count, heads_here, HEAD_DIM)
    )

    def backward_block(totals, block_index):
        grad_key_sum, grad_value_sum = totals
        masked, query_block = block_scores(block_index)
        weights_float = jnp.exp(masked - log_totals[block_index])
        weights_low = weights_float.astype(jnp.bfloat16)
        grad_weights = jnp.einsum(
            "qhd,khd->hqk", grad_context, value_heads, preferred_element_type=jnp.float32
        )
        row_delta = jnp.sum(grad_weights * weights_float, axis=-1, keepdims=True)
        grad_scores = (weights_float * (grad_weights - row_delta)).astype(jnp.bfloat16)
        grad_query_block = (
            jnp.einsum("hqk,khd->qhd", grad_scores, key_heads, preferred_element_type=jnp.float32)
            * scale_factor
        )
        grad_key_sum = (
            grad_key_sum
            + jnp.einsum(
                "hqk,qhd->khd", grad_scores, query_block, preferred_element_type=jnp.float32
            )
            * scale_factor
        )
        grad_value_sum = grad_value_sum + jnp.einsum(
            "hqk,qhd->khd", weights_low, grad_context, preferred_element_type=jnp.float32
        )
        return ((grad_key_sum, grad_value_sum), grad_query_block)

    zero_heads = jnp.zeros((tok_group, heads_here, HEAD_DIM), jnp.float32)
    (grad_key_sum, grad_value_sum), grad_query_blocks = lax.scan(
        backward_block, (zero_heads, zero_heads), jnp.arange(block_count)
    )
    grad_key_flat = grad_key_sum.reshape(tok_group, heads_here * HEAD_DIM)
    grad_value_flat = grad_value_sum.reshape(tok_group, heads_here * HEAD_DIM)
    grad_key_flat = sum_bits(grad_key_flat, low_bits, tensor_index, 0)
    grad_value_flat = sum_bits(grad_value_flat, low_bits, tensor_index, 0)
    grad_queries = grad_query_blocks.reshape(row_count, heads_here * HEAD_DIM).astype(jnp.bfloat16)
    grad_keys = grad_key_flat.astype(jnp.bfloat16)
    grad_values = grad_value_flat.astype(jnp.bfloat16)
    grad_w_query = across_rows(query_rows, grad_queries)
    grad_w_key = across_rows(key_rows, grad_keys)
    grad_w_value = across_rows(value_rows, grad_values)
    grad_w_query = sum_bits(grad_w_query, low_bits, tensor_index, 1)
    grad_w_key = sum_bits(grad_w_key, low_bits, tensor_index, 1)
    grad_w_value = sum_bits(grad_w_value, low_bits, tensor_index, 1)
    grad_w_output = sum_bits(grad_w_output, low_bits, tensor_index, 0)
    stream_partial = jnp.concatenate(
        [
            across_cols(grad_queries, query_whole),
            across_cols(grad_keys, key_whole),
            across_cols(grad_values, value_whole),
        ],
        axis=1,
    )
    grad_streams = sum_bits(stream_partial, high_bits, tensor_index, 0)
    front_grads = front_back(
        (
            grad_streams[:, :model_width],
            grad_streams[:, model_width : 2 * model_width],
            grad_streams[:, 2 * model_width :],
            grad_middle,
        )
    )
    grad_history = front_grads[0].astype(jnp.bfloat16)
    small_sums = lax.psum(
        (
            front_grads[1],
            front_grads[2],
            front_grads[3],
            front_grads[4],
            front_grads[5],
            front_grads[6],
            front_grads[7],
            grad_gain_mlp,
        ),
        ("dp", "tensor"),
    )
    sum_query, sum_key, sum_value, sum_output, sum_expand, sum_reduce = (
        lax.psum_scatter(
            grad_w_query.astype(jnp.bfloat16), "dp", scatter_dimension=0, tiled=True
        ).astype(jnp.float32),
        lax.psum_scatter(
            grad_w_key.astype(jnp.bfloat16), "dp", scatter_dimension=0, tiled=True
        ).astype(jnp.float32),
        lax.psum_scatter(
            grad_w_value.astype(jnp.bfloat16), "dp", scatter_dimension=0, tiled=True
        ).astype(jnp.float32),
        lax.psum_scatter(
            grad_w_output.astype(jnp.bfloat16), "dp", scatter_dimension=1, tiled=True
        ).astype(jnp.float32),
        lax.psum_scatter(
            grad_w_expand.astype(jnp.bfloat16), "dp", scatter_dimension=0, tiled=True
        ).astype(jnp.float32),
        lax.psum_scatter(
            grad_w_reduce.astype(jnp.bfloat16), "dp", scatter_dimension=1, tiled=True
        ).astype(jnp.float32),
    )
    return (
        output,
        grad_history,
        small_sums[0],
        small_sums[1],
        small_sums[2],
        small_sums[3],
        small_sums[4],
        small_sums[5],
        small_sums[6],
        small_sums[7],
        sum_query,
        sum_key,
        sum_value,
        sum_output,
        sum_expand,
        sum_reduce,
    )


def solution(mesh):
    placed = (
        P(None, ("dp", "tensor"), None),
        P(("dp", "tensor"), None),
        P(),
        P(),
        P(),
        P(),
        P(),
        P(),
        P(),
        P(),
        P(),
        P(None, "tensor"),
        P(None, "tensor"),
        P(None, "tensor"),
        P("tensor", None),
        P(None, "tensor"),
        P("tensor", None),
    )
    return jax.shard_map(
        on_device,
        mesh=mesh,
        in_specs=placed,
        out_specs=(
            P(("dp", "tensor"), None),
            P(None, ("dp", "tensor"), None),
            P(),
            P(),
            P(),
            P(),
            P(),
            P(),
            P(),
            P(),
            P("dp", "tensor"),
            P("dp", "tensor"),
            P("dp", "tensor"),
            P("tensor", "dp"),
            P("dp", "tensor"),
            P("tensor", "dp"),
        ),
        check_vma=False,
    )
```

profile of v0, /device:TPU:1, one launch (start us, length us, event | category | flops | bytes accessed | tf_op | source)
XLA Modules:
  0.0 1349.2 jit_solution(5649538605081657744)
XLA Ops:
  16.1 19.8 %fusion.22 = f32[4,128,2048]{2,0,1:T(4,128)S(1)} fusion(f32[128,4,17]{2,1,0:T(4,128)S(1)} %copy.62, bf16[17,128,2048]{2,1,0:T(8,128)(2,1)} %param.17), kind=kOutput, calls=%fused_computation.55 | convolution fusion | flops 213909504 | bytes 13142016 | tf_op jit(solution)/shard_map/jvp(tkj,jtd->ktd)/dot_general | solution.py:35
  51.3 16.1 %collective-permute-done.10 = bf16[128,2048]{1,0:T(8,128)(2,1)} collective-permute-done((bf16[128,2048]{1,0:T(8,128)(2,1)S(1)}, bf16[128,2048]{1,0:T(8,128)(2,1)}, u32[]{:S(2)}, u32[]{:S(2)}) %collective-permute-start.10) | collective-permute-done | bytes 524320 | tf_op jit(solution)/shard_map/ppermute | solution.py:15
  81.2 19.9 %collective-permute-done.6 = bf16[128,2048]{1,0:T(8,128)(2,1)S(1)} collective-permute-done((bf16[128,2048]{1,0:T(8,128)(2,1)S(1)}, bf16[128,2048]{1,0:T(8,128)(2,1)S(1)}, u32[]{:S(2)}, u32[]{:S(2)}) %collective-permute-start.6) | collective-permute-done | bytes 524320 | tf_op jit(solution)/shard_map/ppermute | solution.py:15
  102.9 5.0 convolution_convert_fusion.1
  110.7 13.2 collective-permute-done.3
  132.9 13.5 collective-permute-done.9
  151.4 17.4 %collective-permute-done.15 = bf16[1024,512]{0,1:T(8,128)(2,1)S(1)} collective-permute-done((bf16[1024,512]{0,1:T(8,128)(2,1)S(1)}, bf16[1024,512]{0,1:T(8,128)(2,1)S(1)}, u32[]{:S(2)}, u32[]{:S(2)}) %collective-permute-start.15) | collective-permute-done | bytes 1048608 | tf_op jit(solution)/shard_map/ppermute | solution.py:15
  168.8 8.6 fusion.112
  177.4 8.1 fusion.1
  185.5 28.3 %collective-permute-done.5 = bf16[1024,512]{0,1:T(8,128)(2,1)} collective-permute-done((bf16[1024,512]{0,1:T(8,128)(2,1)}, bf16[1024,512]{0,1:T(8,128)(2,1)}, u32[]{:S(2)}, u32[]{:S(2)}) %collective-permute-start.5) | collective-permute-done | bytes 1048608 | tf_op jit(solution)/shard_map/ppermute | solution.py:15
  213.9 8.3 fusion.30
  227.4 5.1 maximum_select_fusion.2
  233.7 16.4 %collective-permute-done.18 = bf16[256,2048]{1,0:T(8,128)(2,1)S(1)} collective-permute-done((bf16[256,2048]{1,0:T(8,128)(2,1)S(1)}, bf16[256,2048]{1,0:T(8,128)(2,1)S(1)}, u32[]{:S(2)}, u32[]{:S(2)}) %collective-permute-start.18) | collective-permute-done | bytes 1048608 | tf_op jit(solution)/shard_map/ppermute | solution.py:15
  254.3 80.8 %collective-permute-done.19 = bf16[128,2048]{1,0:T(8,128)(2,1)S(1)} collective-permute-done((bf16[128,2048]{1,0:T(8,128)(2,1)S(1)}, bf16[128,2048]{1,0:T(8,128)(2,1)S(1)}, u32[]{:S(2)}, u32[]{:S(2)}) %collective-permute-start.19) | collective-permute-done | bytes 524320 | tf_op jit(solution)/shard_map/ppermute | solution.py:15
  338.4 11.0 collective-permute-done.20
  351.9 3.7 maximum_select_fusion.3
  356.1 5.9 collective-permute-done.28
  366.0 5.8 collective-permute-done.21
  371.8 26.3 %multiply_convert_fusion.1 = (bf16[512,2048]{1,0:T(8,128)(2,1)}, f32[512,2048]{1,0:T(8,128)}, f32[512,2048]{1,0:T(8,128)}) fusion(bf16[2048,1024]{1,0:T(8,128)(2,1)} %copy-done.24, bf16[2048,1024]{1,0:T(8,128)(2,1)} %copy-done.80, pred[]{:T(512)S(6)} %eq.154, bf16[256,2048]{1,0:T(8,128)(2,1)} %copy-done.44, bf16[256,2048]{1,0:T(8,128)(2,1)} %collective-permute-done.21, ...), kind=kOutput, calls=%fused_computation.37 | convolution fusion | flops 4410310656 | bytes 20971522 | tf_op jit(solution)/shard_map/dot_general | solution.py:218
  398.1 52.9 %collective-permute-done.25 = bf16[1024,2048]{1,0:T(8,128)(2,1)} collective-permute-done((bf16[1024,2048]{1,0:T(8,128)(2,1)}, bf16[1024,2048]{1,0:T(8,128)(2,1)}, u32[]{:S(2)}, u32[]{:S(2)}) %collective-permute-start.25) | collective-permute-done | bytes 4194336 | tf_op jit(solution)/shard_map/ppermute | solution.py:15
  451.0 20.3 %add_convert_fusion.2 = bf16[512,2048]{1,0:T(8,128)(2,1)} fusion(f32[512,2048]{1,0:T(8,128)} %get-tuple-element.156, f32[512,2048]{1,0:T(8,128)} %get-tuple-element.171, bf16[1024,2048]{1,0:T(8,128)(2,1)} %maximum_select_fusion.3, bf16[1024,2048]{1,0:T(8,128)(2,1)} %collective-permute-done.25, pred[]{:T(512)S(6)} %eq.154, ...), kind=kOutput, calls=%fused_computation.36 | convolution fusion | flops 4356833280 | bytes 20971522 | tf_op jit(solution)/shard_map/dot_general | solution.py:55
  471.3 10.6 fusion.27
  482.2 10.2 fusion.26
  494.3 7.0 fusion.54
  501.3 34.4 %collective-permute-done.30 = bf16[256,2048]{1,0:T(8,128)(2,1)} collective-permute-done((bf16[256,2048]{1,0:T(8,128)(2,1)S(1)}, bf16[256,2048]{1,0:T(8,128)(2,1)}, u32[]{:S(2)}, u32[]{:S(2)}) %collective-permute-start.30) | collective-permute-done | bytes 1048608 | tf_op jit(solution)/shard_map/ppermute | solution.py:15
  543.8 4.5 collective-permute-done.31
  549.5 10.4 collective-permute-done.27
  566.5 4.8 collective-permute-done.32
  572.9 7.1 fusion.53
  580.0 5.8 copy-done.4
  589.7 4.3 convolution_convert_fusion
  595.0 3.7 fusion.19
  598.7 14.3 %multiply_reduce_fusion = (f32[4,512]{1,0:T(4,128)S(1)}, f32[4,512,2048]{2,1,0:T(8,128)}) fusion(f32[4,512,2048]{2,1,0:T(8,128)} %get-tuple-element.170, f32[4,512]{1,0:T(4,128)S(1)} %log_add_fusion, bf16[512,4,128]{0,2,1:T(8,128)(2,1)S(1)} %bitcast.140, bf16[1024,4,128]{0,2,1:T(8,128)(2,1)S(1)} %copy-done.29, bf16[1024,4,128]{0,2,1:T(8,128)(2,1)} %bitcast.5, ...), kind=kOutput, calls=%fused_computation.3 | convolution fusion | flops 1095759872 | bytes 36192256 | tf_op jit(solution)/shard_map/while/body/eval_jaxpr/qhd,khd->hqk/dot_general | solution.py:252
  613.1 15.9 %multiply_convert_fusion = bf16[4,512,2048]{2,1,0:T(8,128)(2,1)} fusion(f32[4,512,2048]{2,1,0:T(8,128)} %get-tuple-element.173, f32[4,512,2048]{2,1,0:T(8,128)} %get-tuple-element.170, f32[4,512]{1,0:T(4,128)S(1)} %get-tuple-element.172, f32[4,512]{1,0:T(4,128)S(1)} %log_add_fusion), kind=kLoop, calls=%fused_computation.2 | loop fusion | flops 16777216 | bytes 41959424 | tf_op jit(solution)/shard_map/while/body/eval_jaxpr/convert_element_type | solution.py:256
  629.0 6.3 fusion.29
  635.4 4.9 multiply_bitcast_fusion
  651.4 121.1 %collective-permute-done.46 = bf16[256,2048]{1,0:T(8,128)(2,1)S(1)} collective-permute-done((bf16[256,2048]{1,0:T(8,128)(2,1)S(1)}, bf16[256,2048]{1,0:T(8,128)(2,1)S(1)}, u32[]{:S(2)}, u32[]{:S(2)}) %collective-permute-start.46) | collective-permute-done | bytes 1048608 | tf_op jit(solution)/shard_map/ppermute | solution.py:15
  774.2 20.8 %collective-permute-done.36 = bf16[1024,512]{0,1:T(8,128)(2,1)S(1)} collective-permute-done((bf16[1024,512]{0,1:T(8,128)(2,1)S(1)}, bf16[1024,512]{0,1:T(8,128)(2,1)S(1)}, u32[]{:S(2)}, u32[]{:S(2)}) %collective-permute-start.36) | collective-permute-done | bytes 1048608 | tf_op jit(solution)/shard_map/ppermute | solution.py:15
  795.0 12.9 collective-permute-start.47
  809.3 8.2 collective-permute-done.34
  817.5 12.9 collective-permute-start.37
  833.0 7.0 collective-permute-done.40
  840.0 6.7 collective-permute-start.35
  848.4 4.9 convert_add_fusion.1
  862.3 3.7 fusion.63
  870.5 3.7 fusion.59
  882.8 4.6 copy-done.1
  897.2 16.3 %collective-permute-done.42 = bf16[2048,256]{1,0:T(8,128)(2,1)} collective-permute-done((bf16[2048,256]{1,0:T(8,128)(2,1)}, bf16[2048,256]{1,0:T(8,128)(2,1)}, u32[]{:S(2)}, u32[]{:S(2)}) %collective-permute-start.42) | collective-permute-done | bytes 1048608 | tf_op jit(solution)/shard_map/ppermute | solution.py:15
  917.7 11.7 convert_add_fusion
  931.4 5.2 select_convert_fusion.3
  936.7 6.7 add_convert_fusion.1
  943.4 18.8 %collective-permute-done.38 = bf16[256,6144]{1,0:T(8,128)(2,1)} collective-permute-done((bf16[256,6144]{1,0:T(8,128)(2,1)}, bf16[256,6144]{1,0:T(8,128)(2,1)}, u32[]{:S(2)}, u32[]{:S(2)}) %collective-permute-start.38) | collective-permute-done | bytes 3145760 | tf_op jit(solution)/shard_map/ppermute | solution.py:15
  962.2 7.4 convert_add_fusion.2
  976.9 29.3 %reduce-scatter.7.cloned.1.call-done = bf16[256,128]{1,0:T(8,128)(2,1)} async-done(((bf16[2048,128]{1,0:T(8,128)(2,1)}), bf16[256,128]{1,0:T(8,128)(2,1)}) %reduce-scatter.7.cloned.1.call-update) | async-done | bytes 65552 | tf_op jit(solution)/shard_map/reduce_scatter | solution.py:323
  1007.8 6.0 add_convert_fusion
  1014.0 65.8 %reduce-scatter.11.cloned.1.call-done = bf16[256,128]{1,0:T(8,128)(2,1)} async-done(((bf16[2048,128]{1,0:T(8,128)(2,1)}), bf16[256,128]{1,0:T(8,128)(2,1)}) %reduce-scatter.11.cloned.1.call-update) | async-done | bytes 65552 | tf_op jit(solution)/shard_map/reduce_scatter | solution.py:329
  1081.3 71.9 %reduce-scatter.9.cloned.1.call-done = bf16[256,128]{1,0:T(8,128)(2,1)} async-done(((bf16[2048,128]{1,0:T(8,128)(2,1)}), bf16[256,128]{1,0:T(8,128)(2,1)}) %reduce-scatter.9.cloned.1.call-update) | async-done | bytes 65552 | tf_op jit(solution)/shard_map/reduce_scatter | solution.py:326
  1154.8 3.9 convert_add_fusion.3
  1164.7 17.9 %fusion.113 = (f32[4,17]{1,0:T(4,128)S(1)}, f32[128,4,17]{2,1,0:T(4,128)S(1)}) fusion(bf16[17,128,2048]{2,1,0:T(8,128)(2,1)S(1)} %bitcast.136, f32[128,2048,4]{1,0,2:T(8,128)S(1)} %add_bitcast_fusion), kind=kOutput, calls=%fused_computation.270 | convolution fusion | flops 213918144 | bytes 13142288 | tf_op jit(solution)/shard_map/transpose(jvp(tkj,jtd->ktd))/dot_general | solution.py:35
  1190.6 25.6 %fusion = bf16[17,128,2048]{2,0,1:T(8,128)(2,1)} fusion(f32[1,128,2048]{2,0,1:T(1,128)S(1)} %broadcast_in_dim.111, f32[128,4,17]{2,1,0:T(4,128)S(1)} %copy-done.33, f32[128,2048,4]{1,0,2:T(8,128)} %copy-done.25), kind=kOutput, calls=%fused_computation.1 | convolution fusion | flops 222822400 | bytes 14190592 | tf_op jit(solution)/shard_map/transpose(jvp(tkj,jtd->ktd))/dot_general | solution.py:35
  1216.2 13.6 %copy.76 = bf16[17,128,2048]{2,1,0:T(8,128)(2,1)} copy(bf16[17,128,2048]{2,0,1:T(8,128)(2,1)} %fusion) | data formatting | bytes 17825792
  1230.1 69.4 %all-reduce.5 = (f32[2048]{0:T(1024)}, f32[68,68]{1,0:T(8,128)}, f32[68]{0:T(128)}, f32[2048]{0:T(1024)}, f32[2048]{0:T(1024)}, /*index=5*/f32[2048]{0:T(1024)}, f32[2048]{0:T(1024)}) all-reduce(f32[2048]{0:T(1024)S(1)} %get-tuple-element.133, f32[68,68]{1,0:T(8,128)S(1)} %fusion.72, ...), channel_id=1, replica_groups=mesh['dp'=8,'tensor'=16] {'dp','tensor'}, use_global_device_ids=true, to_apply=%region_17.18 | all-reduce | flops 14932 | bytes 119456 | tf_op jit(solution)/shard_map/psum | solution.py:309
  1301.3 8.9 reduce-scatter.17.cloned.1.call-done
  1312.0 27.4 %all-reduce.8.cloned.1.call-done = f32[2048,68]{0,1:T(8,128)} async-done(((f32[2048,68]{0,1:T(8,128)}), f32[2048,68]{0,1:T(8,128)}) %all-reduce.8.cloned.1.call-update) | async-done | bytes 557072 | tf_op jit(solution)/shard_map/psum | solution.py:309
  (424 shorter events, 188.5 us)
Async XLA Ops:
  8.0 967.4 %reduce-scatter.13.cloned.1.call-start = ((), (), s32[]{:S(2)}) async-start(), calls=%async_computation.10 | async-start | bytes 589824 | tf_op jit(solution)/shard_map/reduce_scatter | solution.py:332
  8.1 68.1 %collective-permute-start.8 = (bf16[2048,128]{1,0:T(8,128)(2,1)}, bf16[2048,128]{1,0:T(8,128)(2,1)}, u32[]{:S(2)}, u32[]{:S(2)}) collective-permute-start(bf16[2048,128]{1,0:T(8,128)(2,1)} %param.28), channel_id=1, source_target_pairs={{0,1},{1,0},{2,3},{3,2},{4,5},{5,4},{6,7},{7,6},{8,9},{9,8},{10,11... | collective-permute-start | bytes 1572872 | tf_op jit(solution)/shard_map/ppermute | solution.py:15
  9.6 37.6 %collective-permute-start.12 = (bf16[2048,128]{1,0:T(8,128)(2,1)}, bf16[2048,128]{1,0:T(8,128)(2,1)}, u32[]{:S(2)}, u32[]{:S(2)}) collective-permute-start(bf16[2048,128]{1,0:T(8,128)(2,1)} %param.29), channel_id=1, source_target_pairs={{0,1},{1,0},{2,3},{3,2},{4,5},{5,4},{6,7},{7,6},{8,9},{9,8},{10,11... | collective-permute-start | bytes 1572872 | tf_op jit(solution)/shard_map/ppermute | solution.py:15
  9.7 61.6 %collective-permute-start.2 = (bf16[2048,128]{1,0:T(8,128)(2,1)}, bf16[2048,128]{1,0:T(8,128)(2,1)}, u32[]{:S(2)}, u32[]{:S(2)}) collective-permute-start(bf16[2048,128]{1,0:T(8,128)(2,1)} %param.30), channel_id=1, source_target_pairs={{0,1},{1,0},{2,3},{3,2},{4,5},{5,4},{6,7},{7,6},{8,9},{9,8},{10,11... | collective-permute-start | bytes 1572872 | tf_op jit(solution)/shard_map/ppermute | solution.py:15
  40.5 37.9 %collective-permute-start = (bf16[128,2048]{1,0:T(8,128)(2,1)S(1)}, bf16[128,2048]{1,0:T(8,128)(2,1)}, u32[]{:S(2)}, u32[]{:S(2)}) collective-permute-start(bf16[128,2048]{1,0:T(8,128)(2,1)S(1)} %multiply_convert_fusion.5), channel_id=1, source_target_pairs={{0,4},{1,5},{2,6},{3,7},{4,0},{5,1},{6,2},{7,3},{8,12},{9,13},{10,... | collective-permute-start | bytes 1572872 | tf_op jit(solution)/shard_map/ppermute | solution.py:15
  44.9 22.5 %collective-permute-start.10 = (bf16[128,2048]{1,0:T(8,128)(2,1)S(1)}, bf16[128,2048]{1,0:T(8,128)(2,1)}, u32[]{:S(2)}, u32[]{:S(2)}) collective-permute-start(bf16[128,2048]{1,0:T(8,128)(2,1)S(1)} %multiply_convert_fusion.3), channel_id=1, source_target_pairs={{0,4},{1,5},{2,6},{3,7},{4,0},{5,1},{6,2},{7,3},{8,12},{9,13},{10,... | collective-permute-start | bytes 1572872 | tf_op jit(solution)/shard_map/ppermute | solution.py:15
  50.0 52.6 %collective-permute-start.13 = (bf16[2048,256]{1,0:T(8,128)(2,1)}, bf16[2048,256]{1,0:T(8,128)(2,1)}, u32[]{:S(2)}, u32[]{:S(2)}) collective-permute-start(bf16[2048,256]{1,0:T(8,128)(2,1)} %maximum_select_fusion.29), channel_id=1, source_target_pairs={{0,2},{1,3},{2,0},{3,1},{4,6},{5,7},{6,4},{7,5},{8,10},{9,11},{10,... | collective-permute-start | bytes 3145736 | tf_op jit(solution)/shard_map/ppermute | solution.py:15
  70.0 32.9 %collective-permute-start.11 = (bf16[256,2048]{1,0:T(8,128)(2,1)}, bf16[256,2048]{1,0:T(8,128)(2,1)}, u32[]{:S(2)}, u32[]{:S(2)}) collective-permute-start(bf16[256,2048]{1,0:T(8,128)(2,1)} %maximum_select_fusion.28), channel_id=1, source_target_pairs={{0,8},{1,9},{2,10},{3,11},{4,12},{5,13},{6,14},{7,15},{8,0},{9,1},... | collective-permute-start | bytes 3145736 | tf_op jit(solution)/shard_map/ppermute | solution.py:15
  71.3 29.7 %collective-permute-start.6 = (bf16[128,2048]{1,0:T(8,128)(2,1)S(1)}, bf16[128,2048]{1,0:T(8,128)(2,1)S(1)}, u32[]{:S(2)}, u32[]{:S(2)}) collective-permute-start(bf16[128,2048]{1,0:T(8,128)(2,1)S(1)} %multiply_convert_fusion.4), channel_id=1, source_target_pairs={{0,4},{1,5},{2,6},{3,7},{4,0},{5,1},{6,2},{7,3},{8,12},{9,13},{10,... | collective-permute-start | bytes 1572872 | tf_op jit(solution)/shard_map/ppermute | solution.py:15
  76.1 47.7 %collective-permute-start.3 = (bf16[2048,256]{1,0:T(8,128)(2,1)S(1)}, bf16[2048,256]{1,0:T(8,128)(2,1)S(1)}, u32[]{:S(2)}, u32[]{:S(2)}) collective-permute-start(bf16[2048,256]{1,0:T(8,128)(2,1)S(1)} %maximum_select_fusion.23), channel_id=1, source_target_pairs={{0,2},{1,3},{2,0},{3,1},{4,6},{5,7},{6,4},{7,5},{8,10},{9,11},{10,... | collective-permute-start | bytes 3145736 | tf_op jit(solution)/shard_map/ppermute | solution.py:15
  78.4 69.1 %copy-start.37 = (bf16[2048,256]{1,0:T(8,128)(2,1)}, bf16[2048,256]{1,0:T(8,128)(2,1)S(1)}, u32[]{:S(2)}) copy-start(bf16[2048,256]{1,0:T(8,128)(2,1)S(1)} %maximum_select_fusion.27) | copy-start | bytes 3145732
  78.5 67.9 %collective-permute-start.9 = (bf16[2048,256]{1,0:T(8,128)(2,1)S(1)}, bf16[2048,256]{1,0:T(8,128)(2,1)S(1)}, u32[]{:S(2)}, u32[]{:S(2)}) collective-permute-start(bf16[2048,256]{1,0:T(8,128)(2,1)S(1)} %maximum_select_fusion.27), channel_id=1, source_target_pairs={{0,2},{1,3},{2,0},{3,1},{4,6},{5,7},{6,4},{7,5},{8,10},{9,11},{10,... | collective-permute-start | bytes 3145736 | tf_op jit(solution)/shard_map/ppermute | solution.py:15
  101.0 24.2 %collective-permute-start.1 = (bf16[256,2048]{1,0:T(8,128)(2,1)S(1)}, bf16[256,2048]{1,0:T(8,128)(2,1)S(1)}, u32[]{:S(2)}, u32[]{:S(2)}) collective-permute-start(bf16[256,2048]{1,0:T(8,128)(2,1)S(1)} %maximum_select_fusion.22), channel_id=1, source_target_pairs={{0,8},{1,9},{2,10},{3,11},{4,12},{5,13},{6,14},{7,15},{8,0},{9,1},... | collective-permute-start | bytes 3145736 | tf_op jit(solution)/shard_map/ppermute | solution.py:15
  102.6 45.0 %collective-permute-start.7 = (bf16[256,2048]{1,0:T(8,128)(2,1)S(1)}, bf16[256,2048]{1,0:T(8,128)(2,1)S(1)}, u32[]{:S(2)}, u32[]{:S(2)}) collective-permute-start(bf16[256,2048]{1,0:T(8,128)(2,1)S(1)} %maximum_select_fusion.26), channel_id=1, source_target_pairs={{0,8},{1,9},{2,10},{3,11},{4,12},{5,13},{6,14},{7,15},{8,0},{9,1},... | collective-permute-start | bytes 3145736 | tf_op jit(solution)/shard_map/ppermute | solution.py:15
  107.9 21.9 %collective-permute-start.14 = (bf16[512,512]{0,1:T(8,128)(2,1)S(1)}, bf16[512,512]{0,1:T(8,128)(2,1)S(1)}, u32[]{:S(2)}, u32[]{:S(2)}) collective-permute-start(bf16[512,512]{0,1:T(8,128)(2,1)S(1)} %convolution_convert_fusion.1), channel_id=1, source_target_pairs={{0,1},{1,0},{2,3},{3,2},{4,5},{5,4},{6,7},{7,6},{8,9},{9,8},{10,11... | collective-permute-start | bytes 1572872 | tf_op jit(solution)/shard_map/ppermute | solution.py:15
  123.9 6.3 collective-permute-start.16
  125.2 102.2 %collective-permute-start.22 = (bf16[2048,512]{1,0:T(8,128)(2,1)}, bf16[2048,512]{1,0:T(8,128)(2,1)}, u32[]{:S(2)}, u32[]{:S(2)}) collective-permute-start(bf16[2048,512]{1,0:T(8,128)(2,1)} %param.32), channel_id=1, source_target_pairs={{0,1},{1,0},{2,3},{3,2},{4,5},{5,4},{6,7},{7,6},{8,9},{9,8},{10,11... | collective-permute-start | bytes 6291464 | tf_op jit(solution)/shard_map/ppermute | solution.py:15
  129.8 19.2 %collective-permute-start.4 = (bf16[512,512]{0,1:T(8,128)(2,1)S(1)}, bf16[512,512]{0,1:T(8,128)(2,1)S(1)}, u32[]{:S(2)}, u32[]{:S(2)}) collective-permute-start(bf16[512,512]{0,1:T(8,128)(2,1)S(1)} %convolution_convert_fusion.3), channel_id=1, source_target_pairs={{0,1},{1,0},{2,3},{3,2},{4,5},{5,4},{6,7},{7,6},{8,9},{9,8},{10,11... | collective-permute-start | bytes 1572872 | tf_op jit(solution)/shard_map/ppermute | solution.py:15
  130.2 38.6 %collective-permute-start.15 = (bf16[1024,512]{0,1:T(8,128)(2,1)S(1)}, bf16[1024,512]{0,1:T(8,128)(2,1)S(1)}, u32[]{:S(2)}, u32[]{:S(2)}) collective-permute-start(bf16[1024,512]{0,1:T(8,128)(2,1)S(1)} %maximum_select_fusion.30), channel_id=1, source_target_pairs={{0,2},{1,3},{2,0},{3,1},{4,6},{5,7},{6,4},{7,5},{8,10},{9,11},{10,... | collective-permute-start | bytes 3145736 | tf_op jit(solution)/shard_map/ppermute | solution.py:15
  146.4 75.9 %collective-permute-start.17 = (bf16[256,2048]{1,0:T(8,128)(2,1)}, bf16[256,2048]{1,0:T(8,128)(2,1)}, u32[]{:S(2)}, u32[]{:S(2)}) collective-permute-start(bf16[256,2048]{1,0:T(8,128)(2,1)} %maximum_select_fusion.32), channel_id=1, source_target_pairs={{0,2},{1,3},{2,0},{3,1},{4,6},{5,7},{6,4},{7,5},{8,10},{9,11},{10,... | collective-permute-start | bytes 3145736 | tf_op jit(solution)/shard_map/ppermute | solution.py:15
  150.2 63.7 %collective-permute-start.5 = (bf16[1024,512]{0,1:T(8,128)(2,1)}, bf16[1024,512]{0,1:T(8,128)(2,1)}, u32[]{:S(2)}, u32[]{:S(2)}) collective-permute-start(bf16[1024,512]{0,1:T(8,128)(2,1)} %maximum_select_fusion.24), channel_id=1, source_target_pairs={{0,2},{1,3},{2,0},{3,1},{4,6},{5,7},{6,4},{7,5},{8,10},{9,11},{10,... | collective-permute-start | bytes 3145736 | tf_op jit(solution)/shard_map/ppermute | solution.py:15
  226.1 23.9 %collective-permute-start.18 = (bf16[256,2048]{1,0:T(8,128)(2,1)S(1)}, bf16[256,2048]{1,0:T(8,128)(2,1)S(1)}, u32[]{:S(2)}, u32[]{:S(2)}) collective-permute-start(bf16[256,2048]{1,0:T(8,128)(2,1)S(1)} %select_convert_fusion.14), channel_id=1, source_target_pairs={{0,8},{1,9},{2,10},{3,11},{4,12},{5,13},{6,14},{7,15},{8,0},{9,1},... | collective-permute-start | bytes 3145736 | tf_op jit(solution)/shard_map/ppermute | solution.py:15
  232.5 131.4 %collective-permute-start.23 = (bf16[2048,1024]{1,0:T(8,128)(2,1)S(1)}, bf16[2048,1024]{1,0:T(8,128)(2,1)S(1)}, u32[]{:S(2)}, u32[]{:S(2)}) collective-permute-start(bf16[2048,1024]{1,0:T(8,128)(2,1)S(1)} %maximum_select_fusion.2), channel_id=1, source_target_pairs={{0,2},{1,3},{2,0},{3,1},{4,6},{5,7},{6,4},{7,5},{8,10},{9,11},{10,... | collective-permute-start | bytes 12582920 | tf_op jit(solution)/shard_map/ppermute | solution.py:15
  250.5 85.5 %copy-start.51 = (f32[2048]{0:T(1024)S(1)}, f32[2048]{0:T(1024)}, u32[]{:S(2)}) copy-start(f32[2048]{0:T(1024)} %param.27) | copy-start | bytes 24580
  250.6 84.5 %collective-permute-start.19 = (bf16[128,2048]{1,0:T(8,128)(2,1)S(1)}, bf16[128,2048]{1,0:T(8,128)(2,1)S(1)}, u32[]{:S(2)}, u32[]{:S(2)}) collective-permute-start(bf16[128,2048]{1,0:T(8,128)(2,1)S(1)} %select_convert_fusion.23), channel_id=1, source_target_pairs={{0,4},{1,5},{2,6},{3,7},{4,0},{5,1},{6,2},{7,3},{8,12},{9,13},{10,... | collective-permute-start | bytes 1572872 | tf_op jit(solution)/shard_map/ppermute | solution.py:15
  252.2 99.6 %collective-permute-start.24 = (bf16[512,2048]{1,0:T(8,128)(2,1)S(1)}, bf16[512,2048]{1,0:T(8,128)(2,1)S(1)}, u32[]{:S(2)}, u32[]{:S(2)}) collective-permute-start(bf16[512,2048]{1,0:T(8,128)(2,1)S(1)} %copy-done.31), channel_id=1, source_target_pairs={{0,1},{1,0},{2,3},{3,2},{4,5},{5,4},{6,7},{7,6},{8,9},{9,8},{10,11... | collective-permute-start | bytes 6291464 | tf_op jit(solution)/shard_map/ppermute | solution.py:15
  336.2 13.2 collective-permute-start.20
  349.7 22.1 %collective-permute-start.21 = (bf16[256,2048]{1,0:T(8,128)(2,1)S(1)}, bf16[256,2048]{1,0:T(8,128)(2,1)}, u32[]{:S(2)}, u32[]{:S(2)}) collective-permute-start(bf16[256,2048]{1,0:T(8,128)(2,1)S(1)} %maximum_select_fusion.33), channel_id=1, source_target_pairs={{0,8},{1,9},{2,10},{3,11},{4,12},{5,13},{6,14},{7,15},{8,0},{9,1},... | collective-permute-start | bytes 3145736 | tf_op jit(solution)/shard_map/ppermute | solution.py:15
  350.0 11.9 collective-permute-start.28
  355.6 95.4 %collective-permute-start.25 = (bf16[1024,2048]{1,0:T(8,128)(2,1)}, bf16[1024,2048]{1,0:T(8,128)(2,1)}, u32[]{:S(2)}, u32[]{:S(2)}) collective-permute-start(bf16[1024,2048]{1,0:T(8,128)(2,1)} %maximum_select_fusion.3), channel_id=1, source_target_pairs={{0,2},{1,3},{2,0},{3,1},{4,6},{5,7},{6,4},{7,5},{8,10},{9,11},{10,... | collective-permute-start | bytes 12582920 | tf_op jit(solution)/shard_map/ppermute | solution.py:15
  362.2 88.8 %copy-start.43 = (bf16[256,2048]{1,0:T(8,128)(2,1)}, bf16[256,2048]{1,0:T(8,128)(2,1)S(1)}, u32[]{:S(2)}) copy-start(bf16[256,2048]{1,0:T(8,128)(2,1)S(1)} %maximum_select_fusion.34) | copy-start | bytes 3145732
  362.2 35.9 %collective-permute-start.29 = (bf16[256,2048]{1,0:T(8,128)(2,1)S(1)}, bf16[256,2048]{1,0:T(8,128)(2,1)}, u32[]{:S(2)}, u32[]{:S(2)}) collective-permute-start(bf16[256,2048]{1,0:T(8,128)(2,1)S(1)} %maximum_select_fusion.34), channel_id=1, source_target_pairs={{0,8},{1,9},{2,10},{3,11},{4,12},{5,13},{6,14},{7,15},{8,0},{9,1},... | collective-permute-start | bytes 3145736 | tf_op jit(solution)/shard_map/ppermute | solution.py:15
  492.6 47.8 %collective-permute-start.26 = (bf16[256,2048]{1,0:T(8,128)(2,1)S(1)}, bf16[256,2048]{1,0:T(8,128)(2,1)}, u32[]{:S(2)}, u32[]{:S(2)}) collective-permute-start(bf16[256,2048]{1,0:T(8,128)(2,1)S(1)} %select_convert_fusion.13), channel_id=1, source_target_pairs={{0,8},{1,9},{2,10},{3,11},{4,12},{5,13},{6,14},{7,15},{8,0},{9,1},... | collective-permute-start | bytes 3145736 | tf_op jit(solution)/shard_map/ppermute | solution.py:15
  493.9 41.8 %collective-permute-start.30 = (bf16[256,2048]{1,0:T(8,128)(2,1)S(1)}, bf16[256,2048]{1,0:T(8,128)(2,1)}, u32[]{:S(2)}, u32[]{:S(2)}) collective-permute-start(bf16[256,2048]{1,0:T(8,128)(2,1)S(1)} %select_convert_fusion.12), channel_id=1, source_target_pairs={{0,8},{1,9},{2,10},{3,11},{4,12},{5,13},{6,14},{7,15},{8,0},{9,1},... | collective-permute-start | bytes 3145736 | tf_op jit(solution)/shard_map/ppermute | solution.py:15
  538.8 9.6 collective-permute-start.31
  542.3 17.6 %collective-permute-start.27 = (bf16[128,2048]{1,0:T(8,128)(2,1)S(1)}, bf16[128,2048]{1,0:T(8,128)(2,1)S(1)}, u32[]{:S(2)}, u32[]{:S(2)}) collective-permute-start(bf16[128,2048]{1,0:T(8,128)(2,1)S(1)} %select_convert_fusion.22), channel_id=1, source_target_pairs={{0,4},{1,5},{2,6},{3,7},{4,0},{5,1},{6,2},{7,3},{8,12},{9,13},{10,... | collective-permute-start | bytes 1572872 | tf_op jit(solution)/shard_map/ppermute | solution.py:15
  561.7 9.5 collective-permute-start.32
  565.6 281.5 %collective-permute-start.48 = (bf16[2048,1024]{1,0:T(8,128)(2,1)}, bf16[2048,1024]{1,0:T(8,128)(2,1)}, u32[]{:S(2)}, u32[]{:S(2)}) collective-permute-start(bf16[2048,1024]{1,0:T(8,128)(2,1)} %select_convert_fusion.1), channel_id=1, source_target_pairs={{0,2},{1,3},{2,0},{3,1},{4,6},{5,7},{6,4},{7,5},{8,10},{9,11},{10,... | collective-permute-start | bytes 12582920 | tf_op jit(solution)/shard_map/ppermute | solution.py:15
  571.6 18.2 %collective-permute-start.33 = (bf16[256,2048]{1,0:T(8,128)(2,1)S(1)}, bf16[256,2048]{1,0:T(8,128)(2,1)S(1)}, u32[]{:S(2)}, u32[]{:S(2)}) collective-permute-start(bf16[256,2048]{1,0:T(8,128)(2,1)S(1)} %maximum_select_fusion.35), channel_id=1, source_target_pairs={{0,8},{1,9},{2,10},{3,11},{4,12},{5,13},{6,14},{7,15},{8,0},{9,1},... | collective-permute-start | bytes 3145736 | tf_op jit(solution)/shard_map/ppermute | solution.py:15
  588.3 329.4 %collective-permute-start.50 = (bf16[1024,2048]{1,0:T(8,128)(2,1)}, bf16[1024,2048]{1,0:T(8,128)(2,1)}, u32[]{:S(2)}, u32[]{:S(2)}) collective-permute-start(bf16[1024,2048]{1,0:T(8,128)(2,1)} %select_convert_fusion), channel_id=1, source_target_pairs={{0,2},{1,3},{2,0},{3,1},{4,6},{5,7},{6,4},{7,5},{8,10},{9,11},{10,... | collective-permute-start | bytes 12582920 | tf_op jit(solution)/shard_map/ppermute | solution.py:15
  642.1 130.5 %collective-permute-start.46 = (bf16[256,2048]{1,0:T(8,128)(2,1)S(1)}, bf16[256,2048]{1,0:T(8,128)(2,1)S(1)}, u32[]{:S(2)}, u32[]{:S(2)}) collective-permute-start(bf16[256,2048]{1,0:T(8,128)(2,1)S(1)} %select_convert_fusion.6), channel_id=1, source_target_pairs={{0,2},{1,3},{2,0},{3,1},{4,6},{5,7},{6,4},{7,5},{8,10},{9,11},{10,... | collective-permute-start | bytes 3145736 | tf_op jit(solution)/shard_map/ppermute | solution.py:15
  643.4 151.7 %collective-permute-start.36 = (bf16[1024,512]{0,1:T(8,128)(2,1)S(1)}, bf16[1024,512]{0,1:T(8,128)(2,1)S(1)}, u32[]{:S(2)}, u32[]{:S(2)}) collective-permute-start(bf16[1024,512]{0,1:T(8,128)(2,1)S(1)} %bitcast.146), channel_id=1, source_target_pairs={{0,2},{1,3},{2,0},{3,1},{4,6},{5,7},{6,4},{7,5},{8,10},{9,11},{10,... | collective-permute-start | bytes 3145736 | tf_op jit(solution)/shard_map/ppermute | solution.py:15
  644.1 173.4 %collective-permute-start.34 = (bf16[1024,512]{0,1:T(8,128)(2,1)S(1)}, bf16[1024,512]{0,1:T(8,128)(2,1)S(1)}, u32[]{:S(2)}, u32[]{:S(2)}) collective-permute-start(bf16[1024,512]{0,1:T(8,128)(2,1)S(1)} %bitcast.145), channel_id=1, source_target_pairs={{0,2},{1,3},{2,0},{3,1},{4,6},{5,7},{6,4},{7,5},{8,10},{9,11},{10,... | collective-permute-start | bytes 3145736 | tf_op jit(solution)/shard_map/ppermute | solution.py:15
  772.6 67.4 %collective-permute-start.40 = (bf16[2048,256]{1,0:T(8,128)(2,1)S(1)}, bf16[2048,256]{1,0:T(8,128)(2,1)S(1)}, u32[]{:S(2)}, u32[]{:S(2)}) collective-permute-start(bf16[2048,256]{1,0:T(8,128)(2,1)S(1)} %select_convert_fusion.9), channel_id=1, source_target_pairs={{0,2},{1,3},{2,0},{3,1},{4,6},{5,7},{6,4},{7,5},{8,10},{9,11},{10,... | collective-permute-start | bytes 3145736 | tf_op jit(solution)/shard_map/ppermute | solution.py:15
  772.8 75.5 %slice-start.7 = ((s8[16777216]{0:T(1024)(128)(4,1)}), s8[4194304]{0:T(1024)(128)(4,1)S(1)}, s32[]{:S(2)}) async-start(s8[16777216]{0:T(1024)(128)(4,1)} %bitcast.137), calls=%async_computation.20 | async-start | bytes 8388608
  773.3 75.0 %slice-start.8 = ((s8[16777216]{0:T(1024)(128)(4,1)}), s8[4194304]{0:T(1024)(128)(4,1)S(1)}, s32[]{:S(2)}) async-start(s8[16777216]{0:T(1024)(128)(4,1)} %bitcast.137), calls=%async_computation.21 | async-start | bytes 8388608
  795.0 63.3 %collective-permute-start.47 = (bf16[128,2048]{1,0:T(8,128)(2,1)}, bf16[128,2048]{1,0:T(8,128)(2,1)}, u32[]{:S(2)}, u32[]{:S(2)}) collective-permute-start(bf16[128,2048]{1,0:T(8,128)(2,1)} %select_convert_fusion.15), channel_id=1, source_target_pairs={{0,1},{1,0},{2,3},{3,2},{4,5},{5,4},{6,7},{7,6},{8,9},{9,8},{10,11... | collective-permute-start | bytes 1572872 | tf_op jit(solution)/shard_map/ppermute | solution.py:15
  817.5 43.5 %collective-permute-start.37 = (bf16[512,512]{0,1:T(8,128)(2,1)}, bf16[512,512]{0,1:T(8,128)(2,1)}, u32[]{:S(2)}, u32[]{:S(2)}) collective-permute-start(bf16[512,512]{0,1:T(8,128)(2,1)} %select_convert_fusion.19), channel_id=1, source_target_pairs={{0,1},{1,0},{2,3},{3,2},{4,5},{5,4},{6,7},{7,6},{8,9},{9,8},{10,11... | collective-permute-start | bytes 1572872 | tf_op jit(solution)/shard_map/ppermute | solution.py:15
  840.0 27.3 %collective-permute-start.35 = (bf16[512,512]{0,1:T(8,128)(2,1)}, bf16[512,512]{0,1:T(8,128)(2,1)}, u32[]{:S(2)}, u32[]{:S(2)}) collective-permute-start(bf16[512,512]{0,1:T(8,128)(2,1)} %select_convert_fusion.20), channel_id=1, source_target_pairs={{0,1},{1,0},{2,3},{3,2},{4,5},{5,4},{6,7},{7,6},{8,9},{9,8},{10,11... | collective-permute-start | bytes 1572872 | tf_op jit(solution)/shard_map/ppermute | solution.py:15
  848.3 41.2 %collective-permute-start.41 = (bf16[2048,128]{1,0:T(8,128)(2,1)S(1)}, bf16[2048,128]{1,0:T(8,128)(2,1)}, u32[]{:S(2)}, u32[]{:S(2)}) collective-permute-start(bf16[2048,128]{1,0:T(8,128)(2,1)S(1)} %select_convert_fusion.18), channel_id=1, source_target_pairs={{0,1},{1,0},{2,3},{3,2},{4,5},{5,4},{6,7},{7,6},{8,9},{9,8},{10,11... | collective-permute-start | bytes 1572872 | tf_op jit(solution)/shard_map/ppermute | solution.py:15
  858.3 78.3 %collective-permute-start.49 = (bf16[2048,512]{1,0:T(8,128)(2,1)}, bf16[2048,512]{1,0:T(8,128)(2,1)}, u32[]{:S(2)}, u32[]{:S(2)}) collective-permute-start(bf16[2048,512]{1,0:T(8,128)(2,1)} %select_convert_fusion.4), channel_id=1, source_target_pairs={{0,1},{1,0},{2,3},{3,2},{4,5},{5,4},{6,7},{7,6},{8,9},{9,8},{10,11... | collective-permute-start | bytes 6291464 | tf_op jit(solution)/shard_map/ppermute | solution.py:15
  860.9 145.3 %reduce-scatter.7.cloned.1.call-start = ((), (), s32[]{:S(2)}) async-start(), calls=%async_computation.7 | async-start | bytes 589824 | tf_op jit(solution)/shard_map/reduce_scatter | solution.py:323
  866.2 26.7 %collective-permute-start.44 = (bf16[2048,256]{1,0:T(8,128)(2,1)S(1)}, bf16[2048,256]{1,0:T(8,128)(2,1)}, u32[]{:S(2)}, u32[]{:S(2)}) collective-permute-start(bf16[2048,256]{1,0:T(8,128)(2,1)S(1)} %select_convert_fusion.7), channel_id=1, source_target_pairs={{0,2},{1,3},{2,0},{3,1},{4,6},{5,7},{6,4},{7,5},{8,10},{9,11},{10,... | collective-permute-start | bytes 3145736 | tf_op jit(solution)/shard_map/ppermute | solution.py:15
  875.6 38.0 %collective-permute-start.42 = (bf16[2048,256]{1,0:T(8,128)(2,1)}, bf16[2048,256]{1,0:T(8,128)(2,1)}, u32[]{:S(2)}, u32[]{:S(2)}) collective-permute-start(bf16[2048,256]{1,0:T(8,128)(2,1)} %select_convert_fusion.8), channel_id=1, source_target_pairs={{0,2},{1,3},{2,0},{3,1},{4,6},{5,7},{6,4},{7,5},{8,10},{9,11},{10,... | collective-permute-start | bytes 3145736 | tf_op jit(solution)/shard_map/ppermute | solution.py:15
  889.5 72.7 %collective-permute-start.38 = (bf16[256,6144]{1,0:T(8,128)(2,1)}, bf16[256,6144]{1,0:T(8,128)(2,1)}, u32[]{:S(2)}, u32[]{:S(2)}) collective-permute-start(bf16[256,6144]{1,0:T(8,128)(2,1)} %select_convert_fusion.2), channel_id=1, source_target_pairs={{0,8},{1,9},{2,10},{3,11},{4,12},{5,13},{6,14},{7,15},{8,0},{9,1},... | collective-permute-start | bytes 9437192 | tf_op jit(solution)/shard_map/ppermute | solution.py:15
  892.9 186.9 %reduce-scatter.11.cloned.1.call-start = ((), (), s32[]{:S(2)}) async-start(), calls=%async_computation.9 | async-start | bytes 589824 | tf_op jit(solution)/shard_map/reduce_scatter | solution.py:329
  896.1 20.6 %collective-permute-start.45 = (bf16[2048,128]{1,0:T(8,128)(2,1)S(1)}, bf16[2048,128]{1,0:T(8,128)(2,1)S(1)}, u32[]{:S(2)}, u32[]{:S(2)}) collective-permute-start(bf16[2048,128]{1,0:T(8,128)(2,1)S(1)} %select_convert_fusion.16), channel_id=1, source_target_pairs={{0,1},{1,0},{2,3},{3,2},{4,5},{5,4},{6,7},{7,6},{8,9},{9,8},{10,11... | collective-permute-start | bytes 1572872 | tf_op jit(solution)/shard_map/ppermute | solution.py:15
  915.3 14.1 %collective-permute-start.43 = (bf16[2048,128]{1,0:T(8,128)(2,1)S(1)}, bf16[2048,128]{1,0:T(8,128)(2,1)}, u32[]{:S(2)}, u32[]{:S(2)}) collective-permute-start(bf16[2048,128]{1,0:T(8,128)(2,1)S(1)} %select_convert_fusion.17), channel_id=1, source_target_pairs={{0,1},{1,0},{2,3},{3,2},{4,5},{5,4},{6,7},{7,6},{8,9},{9,8},{10,11... | collective-permute-start | bytes 1572872 | tf_op jit(solution)/shard_map/ppermute | solution.py:15
  917.7 235.6 %reduce-scatter.9.cloned.1.call-start = ((), (), s32[]{:S(2)}) async-start(), calls=%async_computation.8 | async-start | bytes 589824 | tf_op jit(solution)/shard_map/reduce_scatter | solution.py:326
  931.4 368.1 %reduce-scatter.15.cloned.1.call-start = ((), (), s32[]{:S(2)}) async-start(), calls=%async_computation.11 | async-start | bytes 2359296 | tf_op jit(solution)/shard_map/reduce_scatter | solution.py:335
  936.6 71.1 %collective-permute-start.51 = (bf16[512,2048]{1,0:T(8,128)(2,1)}, bf16[512,2048]{1,0:T(8,128)(2,1)S(1)}, u32[]{:S(2)}, u32[]{:S(2)}) collective-permute-start(bf16[512,2048]{1,0:T(8,128)(2,1)} %select_convert_fusion.3), channel_id=1, source_target_pairs={{0,1},{1,0},{2,3},{3,2},{4,5},{5,4},{6,7},{7,6},{8,9},{9,8},{10,11... | collective-permute-start | bytes 6291464 | tf_op jit(solution)/shard_map/ppermute | solution.py:15
  943.3 366.9 %reduce-scatter.17.cloned.1.call-start = ((), (), s32[]{:S(2)}) async-start(), calls=%async_computation.12 | async-start | bytes 2359296 | tf_op jit(solution)/shard_map/reduce_scatter | solution.py:338
  973.8 181.0 %collective-permute-start.39 = (bf16[128,6144]{1,0:T(8,128)(2,1)}, bf16[128,6144]{1,0:T(8,128)(2,1)}, u32[]{:S(2)}, u32[]{:S(2)}) collective-permute-start(bf16[128,6144]{1,0:T(8,128)(2,1)} %select_convert_fusion.5), channel_id=1, source_target_pairs={{0,4},{1,5},{2,6},{3,7},{4,0},{5,1},{6,2},{7,3},{8,12},{9,13},{10,... | collective-permute-start | bytes 4718600 | tf_op jit(solution)/shard_map/ppermute | solution.py:15
  1013.8 325.6 %all-reduce.8.cloned.1.call-start = ((), (), s32[]{:S(2)}) async-start(), calls=%async_computation.6 | async-start | bytes 1179648 | tf_op jit(solution)/shard_map/psum | solution.py:309
  (100 other events, 1016.6 us)
Sparse Core Ops, SparseCore 0:
  861.0 71.6 reduce-scatter.12
  936.8 69.4 reduce-scatter.6
  1010.8 68.9 reduce-scatter.10
  1083.8 69.4 reduce-scatter.8
  1157.3 74.6 reduce-scatter.14
  1235.9 74.2 reduce-scatter.16
Sparse Core Ops, SparseCore 1:
  1190.6 148.7 all-reduce.7
where the time goes:
time: 1350 us
  waiting for transfers between devices  731 us (54%)
  matrix products  235 us (17%)
  other arithmetic  157 us (12%)
  starting transfers between devices  90.5 us (7%)
  blocking collectives  69.4 us (5%)
  local copies, waits for them, and re-layouts  49.2 us (4%)
  between operations  17.8 us (1%)
    ppermute x52, waiting for transfers between devices, swapped(): lax.ppermute(x, axis, [(i, i ^ 1 << bit) for i in range(lax.axis_size(axi...  528 us
    ppermute x52, starting transfers between devices, swapped(): lax.ppermute(x, axis, [(i, i ^ 1 << bit) for i in range(lax.axis_size(axi...  90.1 us
    reduce_scatter x1, waiting for transfers between devices, on_device(): lax.psum_scatter(grad_w_key.astype(jnp.bfloat16), 'dp', scatter_dimension...  71.9 us
    psum x1, blocking collectives, on_device(): lax.psum((front_grads[1], front_grads[2], front_grads[3], front_grads[4],...  69.4 us
    reduce_scatter x1, waiting for transfers between devices, on_device(): lax.psum_scatter(grad_w_value.astype(jnp.bfloat16), 'dp', scatter_dimensi...  65.8 us
    dot_general x3, matrix products, front_part(): jnp.einsum('tkj,jtd->ktd', mixing, history_float, precision=PRECISE)  63.3 us
    unnamed x212, local copies, waits for them, and re-layouts  44.7 us
    dot_general x6, matrix products, across_cols(): lax.dot_general(left_side, right_side, (((1,), (1,)), ((), ())), preferre...  43.8 us
  transfers between devices with their start and end apart: 59, of which 27 were waited for; matrix products, arithmetic and copies ran while one was open for 27% of the time, Pallas kernels for 0%

commit v1 on v0

--- a/solution.py
+++ b/solution.py
@@ -307,17 +307,20 @@
     )
     grad_history = front_grads[0].astype(jnp.bfloat16)
     small_sums = lax.psum(
-        (
-            front_grads[1],
-            front_grads[2],
-            front_grads[3],
-            front_grads[4],
-            front_grads[5],
-            front_grads[6],
-            front_grads[7],
-            grad_gain_mlp,
+        lax.psum(
+            (
+                front_grads[1],
+                front_grads[2],
+                front_grads[3],
+                front_grads[4],
+                front_grads[5],
+                front_grads[6],
+                front_grads[7],
+                grad_gain_mlp,
+            ),
+            "tensor",
         ),
-        ("dp", "tensor"),
+        "dp",
     )
     sum_query, sum_key, sum_value, sum_output, sum_expand, sum_reduce = (
         lax.psum_scatter(

time: 1350 us -> 1410 us (1.044)
  waiting for transfers between devices: 731 us -> 771 us
  blocking collectives: 69.4 us -> 87.1 us
    psum x0 -> x1, waiting for transfers between devices: none -> 82.1 us  [on_device(): lax.psum(lax.psum((front_grads[1], front_grads[2], front_grads[3], front_...]
    ppermute x52, waiting for transfers between devices: 528 us -> 577 us  [swapped(): lax.ppermute(x, axis, [(i, i ^ 1 << bit) for i in range(lax.axis_size(axi...]
    reduce_scatter x1, waiting for transfers between devices: 65.8 us -> 17.3 us  [on_device(): lax.psum_scatter(grad_w_value.astype(jnp.bfloat16), 'dp', scatter_dimensi...]
    psum x0 -> x1, blocking collectives: none -> 34.9 us  [on_device(): lax.psum(lax.psum((front_grads[1], front_grads[2], front_grads[3], front_...]
    reduce_scatter x1, waiting for transfers between devices: 29.3 us -> 0.01 us  [on_device(): lax.psum_scatter(grad_w_query.astype(jnp.bfloat16), 'dp', scatter_dimensi...]
    psum x1, waiting for transfers between devices: 27.4 us -> 0.03 us  [on_device(): lax.psum((front_grads[1], front_grads[2], front_grads[3], front_grads[4],...]
    psum x1, blocking collectives: 69.4 us -> 52.2 us  [on_device(): lax.psum((front_grads[1], front_grads[2], front_grads[3], front_grads[4],...]
    unnamed x212 -> x204, local copies, waits for them, and re-layouts: 44.7 us -> 36.6 us
  transfers between devices with their start and end apart: 59 -> 60, of which waited for: 27 -> 29; matrix products, arithmetic and copies ran while one was open for 27% -> 26% of each run, Pallas kernels for 0% -> 0%
where the time goes in v1:
time: 1410 us; the launch traced here: 1400 us
  waiting for transfers between devices  771 us (55%)
  matrix products  236 us (17%)
  other arithmetic  151 us (11%)
  starting transfers between devices  93.7 us (7%)
  blocking collectives  87.1 us (6%)
  local copies, waits for them, and re-layouts  41 us (3%)
  between operations  17.7 us (1%)
    ppermute x52, waiting for transfers between devices, swapped(): lax.ppermute(x, axis, [(i, i ^ 1 << bit) for i in range(lax.axis_size(axi...  577 us
    ppermute x52, starting transfers between devices, swapped(): lax.ppermute(x, axis, [(i, i ^ 1 << bit) for i in range(lax.axis_size(axi...  92.9 us
    psum x1, waiting for transfers between devices, on_device(): lax.psum(lax.psum((front_grads[1], front_grads[2], front_grads[3], front_...  82.1 us
    reduce_scatter x1, waiting for transfers between devices, on_device(): lax.psum_scatter(grad_w_key.astype(jnp.bfloat16), 'dp', scatter_dimension...  72.7 us
    dot_general x3, matrix products, front_part(): jnp.einsum('tkj,jtd->ktd', mixing, history_float, precision=PRECISE)  63.2 us
    psum x1, blocking collectives, on_device(): lax.psum((front_grads[1], front_grads[2], front_grads[3], front_grads[4],...  52.2 us
    dot_general x6, matrix products, across_cols(): lax.dot_general(left_side, right_side, (((1,), (1,)), ((), ())), preferre...  43.8 us
    add x13, other arithmetic, sum_bits(): keep_half + swapped(send_half.astype(jnp.bfloat16), 'tensor', bit_number)...  38.6 us
  transfers between devices with their start and end apart: 60, of which 29 were waited for; matrix products, arithmetic and copies ran while one was open for 26% of the time, Pallas kernels for 0%

profile of v1, /device:TPU:1, one launch (start us, length us, event | category | flops | bytes accessed | tf_op | source)
XLA Modules:
  0.0 1398.0 jit_solution(2002068263584857788)
XLA Ops:
  16.2 19.8 %fusion.22 = f32[4,128,2048]{2,0,1:T(4,128)S(1)} fusion(f32[128,4,17]{2,1,0:T(4,128)S(1)} %copy.62, bf16[17,128,2048]{2,1,0:T(8,128)(2,1)} %param.17), kind=kOutput, calls=%fused_computation.55 | convolution fusion | flops 213909504 | bytes 13142016 | tf_op jit(solution)/shard_map/jvp(tkj,jtd->ktd)/dot_general | solution.py:35
  51.2 16.2 %collective-permute-done.10 = bf16[128,2048]{1,0:T(8,128)(2,1)} collective-permute-done((bf16[128,2048]{1,0:T(8,128)(2,1)S(1)}, bf16[128,2048]{1,0:T(8,128)(2,1)}, u32[]{:S(2)}, u32[]{:S(2)}) %collective-permute-start.10) | collective-permute-done | bytes 524320 | tf_op jit(solution)/shard_map/ppermute | solution.py:15
  81.2 19.8 %collective-permute-done.6 = bf16[128,2048]{1,0:T(8,128)(2,1)S(1)} collective-permute-done((bf16[128,2048]{1,0:T(8,128)(2,1)S(1)}, bf16[128,2048]{1,0:T(8,128)(2,1)S(1)}, u32[]{:S(2)}, u32[]{:S(2)}) %collective-permute-start.6) | collective-permute-done | bytes 524320 | tf_op jit(solution)/shard_map/ppermute | solution.py:15
  102.8 5.0 convolution_convert_fusion.1
  110.6 13.2 collective-permute-done.3
  132.9 13.5 collective-permute-done.9
  151.4 17.4 %collective-permute-done.15 = bf16[1024,512]{0,1:T(8,128)(2,1)S(1)} collective-permute-done((bf16[1024,512]{0,1:T(8,128)(2,1)S(1)}, bf16[1024,512]{0,1:T(8,128)(2,1)S(1)}, u32[]{:S(2)}, u32[]{:S(2)}) %collective-permute-start.15) | collective-permute-done | bytes 1048608 | tf_op jit(solution)/shard_map/ppermute | solution.py:15
  168.8 8.6 fusion.112
  177.4 8.1 fusion.1
  185.5 28.3 %collective-permute-done.5 = bf16[1024,512]{0,1:T(8,128)(2,1)} collective-permute-done((bf16[1024,512]{0,1:T(8,128)(2,1)}, bf16[1024,512]{0,1:T(8,128)(2,1)}, u32[]{:S(2)}, u32[]{:S(2)}) %collective-permute-start.5) | collective-permute-done | bytes 1048608 | tf_op jit(solution)/shard_map/ppermute | solution.py:15
  213.8 8.3 fusion.30
  227.4 5.1 maximum_select_fusion.2
  233.6 16.3 %collective-permute-done.18 = bf16[256,2048]{1,0:T(8,128)(2,1)S(1)} collective-permute-done((bf16[256,2048]{1,0:T(8,128)(2,1)S(1)}, bf16[256,2048]{1,0:T(8,128)(2,1)S(1)}, u32[]{:S(2)}, u32[]{:S(2)}) %collective-permute-start.18) | collective-permute-done | bytes 1048608 | tf_op jit(solution)/shard_map/ppermute | solution.py:15
  254.2 80.9 %collective-permute-done.19 = bf16[128,2048]{1,0:T(8,128)(2,1)S(1)} collective-permute-done((bf16[128,2048]{1,0:T(8,128)(2,1)S(1)}, bf16[128,2048]{1,0:T(8,128)(2,1)S(1)}, u32[]{:S(2)}, u32[]{:S(2)}) %collective-permute-start.19) | collective-permute-done | bytes 524320 | tf_op jit(solution)/shard_map/ppermute | solution.py:15
  338.4 11.0 collective-permute-done.20
  351.9 3.7 maximum_select_fusion.3
  356.0 6.0 collective-permute-done.28
  366.0 5.8 collective-permute-done.21
  371.8 26.4 %multiply_convert_fusion.1 = (bf16[512,2048]{1,0:T(8,128)(2,1)}, f32[512,2048]{1,0:T(8,128)}, f32[512,2048]{1,0:T(8,128)}) fusion(bf16[2048,1024]{1,0:T(8,128)(2,1)} %copy-done.19, bf16[2048,1024]{1,0:T(8,128)(2,1)} %copy-done.76, pred[]{:T(512)S(6)} %eq.154, bf16[256,2048]{1,0:T(8,128)(2,1)} %copy-done.38, bf16[256,2048]{1,0:T(8,128)(2,1)} %collective-permute-done.21, ...), kind=kOutput, calls=%fused_computation.37 | convolution fusion | flops 4410310656 | bytes 20971522 | tf_op jit(solution)/shard_map/dot_general | solution.py:218
  398.3 52.6 %collective-permute-done.25 = bf16[1024,2048]{1,0:T(8,128)(2,1)} collective-permute-done((bf16[1024,2048]{1,0:T(8,128)(2,1)}, bf16[1024,2048]{1,0:T(8,128)(2,1)}, u32[]{:S(2)}, u32[]{:S(2)}) %collective-permute-start.25) | collective-permute-done | bytes 4194336 | tf_op jit(solution)/shard_map/ppermute | solution.py:15
  450.9 20.4 %add_convert_fusion.2 = bf16[512,2048]{1,0:T(8,128)(2,1)} fusion(f32[512,2048]{1,0:T(8,128)} %get-tuple-element.163, f32[512,2048]{1,0:T(8,128)} %get-tuple-element.178, bf16[1024,2048]{1,0:T(8,128)(2,1)} %maximum_select_fusion.3, bf16[1024,2048]{1,0:T(8,128)(2,1)} %collective-permute-done.25, pred[]{:T(512)S(6)} %eq.154, ...), kind=kOutput, calls=%fused_computation.36 | convolution fusion | flops 4356833280 | bytes 20971522 | tf_op jit(solution)/shard_map/dot_general | solution.py:55
  471.2 10.6 fusion.27
  482.1 10.2 fusion.26
  494.2 7.0 fusion.54
  501.2 34.3 %collective-permute-done.30 = bf16[256,2048]{1,0:T(8,128)(2,1)} collective-permute-done((bf16[256,2048]{1,0:T(8,128)(2,1)S(1)}, bf16[256,2048]{1,0:T(8,128)(2,1)}, u32[]{:S(2)}, u32[]{:S(2)}) %collective-permute-start.30) | collective-permute-done | bytes 1048608 | tf_op jit(solution)/shard_map/ppermute | solution.py:15
  543.8 4.5 collective-permute-done.31
  549.4 10.4 collective-permute-done.27
  566.6 4.6 collective-permute-done.32
  572.9 7.2 fusion.53
  580.1 5.8 copy-done.3
  589.9 4.3 convolution_convert_fusion
  595.1 3.7 fusion.19
  598.8 14.3 %multiply_reduce_fusion = (f32[4,512]{1,0:T(4,128)S(1)}, f32[4,512,2048]{2,1,0:T(8,128)}) fusion(f32[4,512,2048]{2,1,0:T(8,128)} %get-tuple-element.177, f32[4,512]{1,0:T(4,128)S(1)} %log_add_fusion, bf16[512,4,128]{0,2,1:T(8,128)(2,1)S(1)} %bitcast.140, bf16[1024,4,128]{0,2,1:T(8,128)(2,1)S(1)} %copy-done.23, bf16[1024,4,128]{0,2,1:T(8,128)(2,1)} %bitcast.5, ...), kind=kOutput, calls=%fused_computation.3 | convolution fusion | flops 1095759872 | bytes 36192256 | tf_op jit(solution)/shard_map/while/body/eval_jaxpr/qhd,khd->hqk/dot_general | solution.py:252
  613.1 15.9 %multiply_convert_fusion = bf16[4,512,2048]{2,1,0:T(8,128)(2,1)} fusion(f32[4,512,2048]{2,1,0:T(8,128)} %get-tuple-element.180, f32[4,512,2048]{2,1,0:T(8,128)} %get-tuple-element.177, f32[4,512]{1,0:T(4,128)S(1)} %get-tuple-element.179, f32[4,512]{1,0:T(4,128)S(1)} %log_add_fusion), kind=kLoop, calls=%fused_computation.2 | loop fusion | flops 16777216 | bytes 41959424 | tf_op jit(solution)/shard_map/while/body/eval_jaxpr/convert_element_type | solution.py:256
  629.0 6.3 fusion.29
  635.4 4.9 multiply_bitcast_fusion
  651.3 121.4 %collective-permute-done.46 = bf16[256,2048]{1,0:T(8,128)(2,1)S(1)} collective-permute-done((bf16[256,2048]{1,0:T(8,128)(2,1)S(1)}, bf16[256,2048]{1,0:T(8,128)(2,1)S(1)}, u32[]{:S(2)}, u32[]{:S(2)}) %collective-permute-start.46) | collective-permute-done | bytes 1048608 | tf_op jit(solution)/shard_map/ppermute | solution.py:15
  773.5 21.6 %collective-permute-done.36 = bf16[1024,512]{0,1:T(8,128)(2,1)S(1)} collective-permute-done((bf16[1024,512]{0,1:T(8,128)(2,1)S(1)}, bf16[1024,512]{0,1:T(8,128)(2,1)S(1)}, u32[]{:S(2)}, u32[]{:S(2)}) %collective-permute-start.36) | collective-permute-done | bytes 1048608 | tf_op jit(solution)/shard_map/ppermute | solution.py:15
  795.1 12.9 collective-permute-start.47
  809.4 8.2 collective-permute-done.34
  817.6 12.9 collective-permute-start.37
  831.8 8.3 collective-permute-done.40
  840.1 6.7 collective-permute-start.35
  847.3 7.4 convert_add_fusion.1
  858.8 3.8 fusion.63
  879.2 5.3 fusion.59
  895.4 18.2 %collective-permute-done.42 = bf16[2048,256]{1,0:T(8,128)(2,1)} collective-permute-done((bf16[2048,256]{1,0:T(8,128)(2,1)S(1)}, bf16[2048,256]{1,0:T(8,128)(2,1)}, u32[]{:S(2)}, u32[]{:S(2)}) %collective-permute-start.42) | collective-permute-done | bytes 1048608 | tf_op jit(solution)/shard_map/ppermute | solution.py:15
  916.2 34.8 %collective-permute-done.38 = bf16[256,6144]{1,0:T(8,128)(2,1)} collective-permute-done((bf16[256,6144]{1,0:T(8,128)(2,1)}, bf16[256,6144]{1,0:T(8,128)(2,1)}, u32[]{:S(2)}, u32[]{:S(2)}) %collective-permute-start.38) | collective-permute-done | bytes 3145760 | tf_op jit(solution)/shard_map/ppermute | solution.py:15
  951.0 7.4 convert_add_fusion.2
  965.5 5.2 select_convert_fusion.4
  974.3 24.9 %collective-permute-done.39 = bf16[128,6144]{1,0:T(8,128)(2,1)} collective-permute-done((bf16[128,6144]{1,0:T(8,128)(2,1)}, bf16[128,6144]{1,0:T(8,128)(2,1)}, u32[]{:S(2)}, u32[]{:S(2)}) %collective-permute-start.39) | collective-permute-done | bytes 1572896 | tf_op jit(solution)/shard_map/ppermute | solution.py:15
  999.2 3.8 convert_add_fusion.3
  1008.9 17.9 %fusion.113 = (f32[4,17]{1,0:T(4,128)S(1)}, f32[128,4,17]{2,1,0:T(4,128)S(1)}) fusion(bf16[17,128,2048]{2,1,0:T(8,128)(2,1)S(1)} %bitcast.136, f32[128,2048,4]{1,0,2:T(8,128)S(1)} %add_bitcast_fusion), kind=kOutput, calls=%fused_computation.270 | convolution fusion | flops 213918144 | bytes 13142288 | tf_op jit(solution)/shard_map/transpose(jvp(tkj,jtd->ktd))/dot_general | solution.py:35
  1030.2 6.7 add_convert_fusion.1
  1037.0 8.7 convert_add_fusion
  1048.0 3.8 collective-permute-done.51
  1057.5 17.3 %reduce-scatter.11.cloned.1.call-done = bf16[256,128]{1,0:T(8,128)(2,1)} async-done(((bf16[2048,128]{1,0:T(8,128)(2,1)}), bf16[256,128]{1,0:T(8,128)(2,1)}) %reduce-scatter.11.cloned.1.call-update) | async-done | bytes 65552 | tf_op jit(solution)/shard_map/reduce_scatter | solution.py:332
  1076.2 72.7 %reduce-scatter.9.cloned.1.call-done = bf16[256,128]{1,0:T(8,128)(2,1)} async-done(((bf16[2048,128]{1,0:T(8,128)(2,1)}), bf16[256,128]{1,0:T(8,128)(2,1)}) %reduce-scatter.9.cloned.1.call-update) | async-done | bytes 65552 | tf_op jit(solution)/shard_map/reduce_scatter | solution.py:329
  1155.0 25.5 %fusion = bf16[17,128,2048]{2,0,1:T(8,128)(2,1)} fusion(f32[1,128,2048]{2,0,1:T(1,128)S(1)} %broadcast_in_dim.111, f32[128,4,17]{2,1,0:T(4,128)S(1)} %copy-done.27, f32[128,2048,4]{1,0,2:T(8,128)} %copy-done.18), kind=kOutput, calls=%fused_computation.1 | convolution fusion | flops 222822400 | bytes 14190592 | tf_op jit(solution)/shard_map/transpose(jvp(tkj,jtd->ktd))/dot_general | solution.py:35
  1180.7 13.5 copy.76
  1194.5 52.2 %all-reduce.5 = (f32[2048]{0:T(1024)S(1)}, f32[68,68]{1,0:T(8,128)S(1)}, f32[68]{0:T(128)S(1)}, f32[2048]{0:T(1024)S(1)}, f32[2048]{0:T(1024)S(1)}, /*index=5*/f32[2048]{0:T(1024)S(1)}, f32[2048]{0:T(1024)S(1)}) all-reduce(f32[2048]{0:T(1024)S(1)} %get-tuple-element.133, ...), channel_id=1, replica_groups=mesh['dp'=8,'tensor'=16] {'tensor'}, use_global_device_ids=true, to_apply=%region_17.18 | all-reduce | flops 14932 | bytes 119456 | tf_op jit(solution)/shard_map/psum | solution.py:310
  1246.7 34.9 %all-reduce.6 = (f32[2048]{0:T(1024)}, f32[68,68]{1,0:T(8,128)}, f32[68]{0:T(128)}, f32[2048]{0:T(1024)}, f32[2048]{0:T(1024)}, /*index=5*/f32[2048]{0:T(1024)}, f32[2048]{0:T(1024)}) all-reduce(f32[2048]{0:T(1024)S(1)} %get-tuple-element.147, f32[68,68]{1,0:T(8,128)S(1)} %get-tuple-element.148, ...), channel_id=1, replica_groups=mesh['dp'=8,'tensor'=16] {'dp'}, use_global_device_ids=true, to_apply=%region_18.19 | all-reduce | flops 14932 | bytes 119456 | tf_op jit(solution)/shard_map/psum | solution.py:309
  1283.4 21.2 %reduce-scatter.17.cloned.1.call-done = bf16[512,256]{1,0:T(8,128)(2,1)} async-done(((bf16[512,2048]{1,0:T(8,128)(2,1)}), bf16[512,256]{1,0:T(8,128)(2,1)}) %reduce-scatter.17.cloned.1.call-update) | async-done | bytes 262160 | tf_op jit(solution)/shard_map/reduce_scatter | solution.py:341
  1306.3 82.1 %all-reduce.12.cloned.1.call-done = f32[2048,68]{0,1:T(8,128)} async-done(((f32[2048,68]{0,1:T(8,128)}), f32[2048,68]{0,1:T(8,128)}) %all-reduce.12.cloned.1.call-update) | async-done | bytes 557072 | tf_op jit(solution)/shard_map/psum | solution.py:309
  (420 shorter events, 190.6 us)
Async XLA Ops:
  8.0 1046.4 %reduce-scatter.13.cloned.1.call-start = ((), (), s32[]{:S(2)}) async-start(), calls=%async_computation.11 | async-start | bytes 589824 | tf_op jit(solution)/shard_map/reduce_scatter | solution.py:335
  8.1 68.0 %collective-permute-start.8 = (bf16[2048,128]{1,0:T(8,128)(2,1)}, bf16[2048,128]{1,0:T(8,128)(2,1)}, u32[]{:S(2)}, u32[]{:S(2)}) collective-permute-start(bf16[2048,128]{1,0:T(8,128)(2,1)} %param.28), channel_id=1, source_target_pairs={{0,1},{1,0},{2,3},{3,2},{4,5},{5,4},{6,7},{7,6},{8,9},{9,8},{10,11... | collective-permute-start | bytes 1572872 | tf_op jit(solution)/shard_map/ppermute | solution.py:15
  9.6 37.5 %collective-permute-start.12 = (bf16[2048,128]{1,0:T(8,128)(2,1)}, bf16[2048,128]{1,0:T(8,128)(2,1)}, u32[]{:S(2)}, u32[]{:S(2)}) collective-permute-start(bf16[2048,128]{1,0:T(8,128)(2,1)} %param.29), channel_id=1, source_target_pairs={{0,1},{1,0},{2,3},{3,2},{4,5},{5,4},{6,7},{7,6},{8,9},{9,8},{10,11... | collective-permute-start | bytes 1572872 | tf_op jit(solution)/shard_map/ppermute | solution.py:15
  9.7 61.6 %collective-permute-start.2 = (bf16[2048,128]{1,0:T(8,128)(2,1)}, bf16[2048,128]{1,0:T(8,128)(2,1)}, u32[]{:S(2)}, u32[]{:S(2)}) collective-permute-start(bf16[2048,128]{1,0:T(8,128)(2,1)} %param.30), channel_id=1, source_target_pairs={{0,1},{1,0},{2,3},{3,2},{4,5},{5,4},{6,7},{7,6},{8,9},{9,8},{10,11... | collective-permute-start | bytes 1572872 | tf_op jit(solution)/shard_map/ppermute | solution.py:15
  40.5 37.9 %collective-permute-start = (bf16[128,2048]{1,0:T(8,128)(2,1)S(1)}, bf16[128,2048]{1,0:T(8,128)(2,1)}, u32[]{:S(2)}, u32[]{:S(2)}) collective-permute-start(bf16[128,2048]{1,0:T(8,128)(2,1)S(1)} %multiply_convert_fusion.5), channel_id=1, source_target_pairs={{0,4},{1,5},{2,6},{3,7},{4,0},{5,1},{6,2},{7,3},{8,12},{9,13},{10,... | collective-permute-start | bytes 1572872 | tf_op jit(solution)/shard_map/ppermute | solution.py:15
  44.9 22.5 %collective-permute-start.10 = (bf16[128,2048]{1,0:T(8,128)(2,1)S(1)}, bf16[128,2048]{1,0:T(8,128)(2,1)}, u32[]{:S(2)}, u32[]{:S(2)}) collective-permute-start(bf16[128,2048]{1,0:T(8,128)(2,1)S(1)} %multiply_convert_fusion.3), channel_id=1, source_target_pairs={{0,4},{1,5},{2,6},{3,7},{4,0},{5,1},{6,2},{7,3},{8,12},{9,13},{10,... | collective-permute-start | bytes 1572872 | tf_op jit(solution)/shard_map/ppermute | solution.py:15
  49.8 52.7 %collective-permute-start.13 = (bf16[2048,256]{1,0:T(8,128)(2,1)}, bf16[2048,256]{1,0:T(8,128)(2,1)}, u32[]{:S(2)}, u32[]{:S(2)}) collective-permute-start(bf16[2048,256]{1,0:T(8,128)(2,1)} %maximum_select_fusion.29), channel_id=1, source_target_pairs={{0,2},{1,3},{2,0},{3,1},{4,6},{5,7},{6,4},{7,5},{8,10},{9,11},{10,... | collective-permute-start | bytes 3145736 | tf_op jit(solution)/shard_map/ppermute | solution.py:15
  69.9 32.9 %collective-permute-start.11 = (bf16[256,2048]{1,0:T(8,128)(2,1)}, bf16[256,2048]{1,0:T(8,128)(2,1)}, u32[]{:S(2)}, u32[]{:S(2)}) collective-permute-start(bf16[256,2048]{1,0:T(8,128)(2,1)} %maximum_select_fusion.28), channel_id=1, source_target_pairs={{0,8},{1,9},{2,10},{3,11},{4,12},{5,13},{6,14},{7,15},{8,0},{9,1},... | collective-permute-start | bytes 3145736 | tf_op jit(solution)/shard_map/ppermute | solution.py:15
  71.3 29.7 %collective-permute-start.6 = (bf16[128,2048]{1,0:T(8,128)(2,1)S(1)}, bf16[128,2048]{1,0:T(8,128)(2,1)S(1)}, u32[]{:S(2)}, u32[]{:S(2)}) collective-permute-start(bf16[128,2048]{1,0:T(8,128)(2,1)S(1)} %multiply_convert_fusion.4), channel_id=1, source_target_pairs={{0,4},{1,5},{2,6},{3,7},{4,0},{5,1},{6,2},{7,3},{8,12},{9,13},{10,... | collective-permute-start | bytes 1572872 | tf_op jit(solution)/shard_map/ppermute | solution.py:15
  76.1 47.7 %collective-permute-start.3 = (bf16[2048,256]{1,0:T(8,128)(2,1)S(1)}, bf16[2048,256]{1,0:T(8,128)(2,1)S(1)}, u32[]{:S(2)}, u32[]{:S(2)}) collective-permute-start(bf16[2048,256]{1,0:T(8,128)(2,1)S(1)} %maximum_select_fusion.23), channel_id=1, source_target_pairs={{0,2},{1,3},{2,0},{3,1},{4,6},{5,7},{6,4},{7,5},{8,10},{9,11},{10,... | collective-permute-start | bytes 3145736 | tf_op jit(solution)/shard_map/ppermute | solution.py:15
  78.5 67.8 %collective-permute-start.9 = (bf16[2048,256]{1,0:T(8,128)(2,1)S(1)}, bf16[2048,256]{1,0:T(8,128)(2,1)S(1)}, u32[]{:S(2)}, u32[]{:S(2)}) collective-permute-start(bf16[2048,256]{1,0:T(8,128)(2,1)S(1)} %maximum_select_fusion.27), channel_id=1, source_target_pairs={{0,2},{1,3},{2,0},{3,1},{4,6},{5,7},{6,4},{7,5},{8,10},{9,11},{10,... | collective-permute-start | bytes 3145736 | tf_op jit(solution)/shard_map/ppermute | solution.py:15
  101.0 24.2 %collective-permute-start.1 = (bf16[256,2048]{1,0:T(8,128)(2,1)S(1)}, bf16[256,2048]{1,0:T(8,128)(2,1)S(1)}, u32[]{:S(2)}, u32[]{:S(2)}) collective-permute-start(bf16[256,2048]{1,0:T(8,128)(2,1)S(1)} %maximum_select_fusion.22), channel_id=1, source_target_pairs={{0,8},{1,9},{2,10},{3,11},{4,12},{5,13},{6,14},{7,15},{8,0},{9,1},... | collective-permute-start | bytes 3145736 | tf_op jit(solution)/shard_map/ppermute | solution.py:15
  102.5 45.0 %collective-permute-start.7 = (bf16[256,2048]{1,0:T(8,128)(2,1)S(1)}, bf16[256,2048]{1,0:T(8,128)(2,1)S(1)}, u32[]{:S(2)}, u32[]{:S(2)}) collective-permute-start(bf16[256,2048]{1,0:T(8,128)(2,1)S(1)} %maximum_select_fusion.26), channel_id=1, source_target_pairs={{0,8},{1,9},{2,10},{3,11},{4,12},{5,13},{6,14},{7,15},{8,0},{9,1},... | collective-permute-start | bytes 3145736 | tf_op jit(solution)/shard_map/ppermute | solution.py:15
  107.8 21.9 %collective-permute-start.14 = (bf16[512,512]{0,1:T(8,128)(2,1)S(1)}, bf16[512,512]{0,1:T(8,128)(2,1)S(1)}, u32[]{:S(2)}, u32[]{:S(2)}) collective-permute-start(bf16[512,512]{0,1:T(8,128)(2,1)S(1)} %convolution_convert_fusion.1), channel_id=1, source_target_pairs={{0,1},{1,0},{2,3},{3,2},{4,5},{5,4},{6,7},{7,6},{8,9},{9,8},{10,11... | collective-permute-start | bytes 1572872 | tf_op jit(solution)/shard_map/ppermute | solution.py:15
  123.8 6.3 collective-permute-start.16
  125.2 102.2 %collective-permute-start.22 = (bf16[2048,512]{1,0:T(8,128)(2,1)}, bf16[2048,512]{1,0:T(8,128)(2,1)}, u32[]{:S(2)}, u32[]{:S(2)}) collective-permute-start(bf16[2048,512]{1,0:T(8,128)(2,1)} %param.32), channel_id=1, source_target_pairs={{0,1},{1,0},{2,3},{3,2},{4,5},{5,4},{6,7},{7,6},{8,9},{9,8},{10,11... | collective-permute-start | bytes 6291464 | tf_op jit(solution)/shard_map/ppermute | solution.py:15
  129.7 19.2 %collective-permute-start.4 = (bf16[512,512]{0,1:T(8,128)(2,1)S(1)}, bf16[512,512]{0,1:T(8,128)(2,1)S(1)}, u32[]{:S(2)}, u32[]{:S(2)}) collective-permute-start(bf16[512,512]{0,1:T(8,128)(2,1)S(1)} %convolution_convert_fusion.3), channel_id=1, source_target_pairs={{0,1},{1,0},{2,3},{3,2},{4,5},{5,4},{6,7},{7,6},{8,9},{9,8},{10,11... | collective-permute-start | bytes 1572872 | tf_op jit(solution)/shard_map/ppermute | solution.py:15
  130.1 38.6 %collective-permute-start.15 = (bf16[1024,512]{0,1:T(8,128)(2,1)S(1)}, bf16[1024,512]{0,1:T(8,128)(2,1)S(1)}, u32[]{:S(2)}, u32[]{:S(2)}) collective-permute-start(bf16[1024,512]{0,1:T(8,128)(2,1)S(1)} %maximum_select_fusion.30), channel_id=1, source_target_pairs={{0,2},{1,3},{2,0},{3,1},{4,6},{5,7},{6,4},{7,5},{8,10},{9,11},{10,... | collective-permute-start | bytes 3145736 | tf_op jit(solution)/shard_map/ppermute | solution.py:15
  146.3 75.9 %collective-permute-start.17 = (bf16[256,2048]{1,0:T(8,128)(2,1)}, bf16[256,2048]{1,0:T(8,128)(2,1)}, u32[]{:S(2)}, u32[]{:S(2)}) collective-permute-start(bf16[256,2048]{1,0:T(8,128)(2,1)} %maximum_select_fusion.32), channel_id=1, source_target_pairs={{0,2},{1,3},{2,0},{3,1},{4,6},{5,7},{6,4},{7,5},{8,10},{9,11},{10,... | collective-permute-start | bytes 3145736 | tf_op jit(solution)/shard_map/ppermute | solution.py:15
  150.2 63.7 %collective-permute-start.5 = (bf16[1024,512]{0,1:T(8,128)(2,1)}, bf16[1024,512]{0,1:T(8,128)(2,1)}, u32[]{:S(2)}, u32[]{:S(2)}) collective-permute-start(bf16[1024,512]{0,1:T(8,128)(2,1)} %maximum_select_fusion.24), channel_id=1, source_target_pairs={{0,2},{1,3},{2,0},{3,1},{4,6},{5,7},{6,4},{7,5},{8,10},{9,11},{10,... | collective-permute-start | bytes 3145736 | tf_op jit(solution)/shard_map/ppermute | solution.py:15
  226.1 23.9 %collective-permute-start.18 = (bf16[256,2048]{1,0:T(8,128)(2,1)S(1)}, bf16[256,2048]{1,0:T(8,128)(2,1)S(1)}, u32[]{:S(2)}, u32[]{:S(2)}) collective-permute-start(bf16[256,2048]{1,0:T(8,128)(2,1)S(1)} %select_convert_fusion.14), channel_id=1, source_target_pairs={{0,8},{1,9},{2,10},{3,11},{4,12},{5,13},{6,14},{7,15},{8,0},{9,1},... | collective-permute-start | bytes 3145736 | tf_op jit(solution)/shard_map/ppermute | solution.py:15
  232.5 131.5 %collective-permute-start.23 = (bf16[2048,1024]{1,0:T(8,128)(2,1)S(1)}, bf16[2048,1024]{1,0:T(8,128)(2,1)S(1)}, u32[]{:S(2)}, u32[]{:S(2)}) collective-permute-start(bf16[2048,1024]{1,0:T(8,128)(2,1)S(1)} %maximum_select_fusion.2), channel_id=1, source_target_pairs={{0,2},{1,3},{2,0},{3,1},{4,6},{5,7},{6,4},{7,5},{8,10},{9,11},{10,... | collective-permute-start | bytes 12582920 | tf_op jit(solution)/shard_map/ppermute | solution.py:15
  250.4 85.6 %copy-start.47 = (f32[2048]{0:T(1024)S(1)}, f32[2048]{0:T(1024)}, u32[]{:S(2)}) copy-start(f32[2048]{0:T(1024)} %param.27) | copy-start | bytes 24580
  250.5 84.6 %collective-permute-start.19 = (bf16[128,2048]{1,0:T(8,128)(2,1)S(1)}, bf16[128,2048]{1,0:T(8,128)(2,1)S(1)}, u32[]{:S(2)}, u32[]{:S(2)}) collective-permute-start(bf16[128,2048]{1,0:T(8,128)(2,1)S(1)} %select_convert_fusion.23), channel_id=1, source_target_pairs={{0,4},{1,5},{2,6},{3,7},{4,0},{5,1},{6,2},{7,3},{8,12},{9,13},{10,... | collective-permute-start | bytes 1572872 | tf_op jit(solution)/shard_map/ppermute | solution.py:15
  252.2 99.7 %collective-permute-start.24 = (bf16[512,2048]{1,0:T(8,128)(2,1)S(1)}, bf16[512,2048]{1,0:T(8,128)(2,1)S(1)}, u32[]{:S(2)}, u32[]{:S(2)}) collective-permute-start(bf16[512,2048]{1,0:T(8,128)(2,1)S(1)} %copy-done.25), channel_id=1, source_target_pairs={{0,1},{1,0},{2,3},{3,2},{4,5},{5,4},{6,7},{7,6},{8,9},{9,8},{10,11... | collective-permute-start | bytes 6291464 | tf_op jit(solution)/shard_map/ppermute | solution.py:15
  336.2 13.2 collective-permute-start.20
  349.7 22.1 %collective-permute-start.21 = (bf16[256,2048]{1,0:T(8,128)(2,1)S(1)}, bf16[256,2048]{1,0:T(8,128)(2,1)}, u32[]{:S(2)}, u32[]{:S(2)}) collective-permute-start(bf16[256,2048]{1,0:T(8,128)(2,1)S(1)} %maximum_select_fusion.33), channel_id=1, source_target_pairs={{0,8},{1,9},{2,10},{3,11},{4,12},{5,13},{6,14},{7,15},{8,0},{9,1},... | collective-permute-start | bytes 3145736 | tf_op jit(solution)/shard_map/ppermute | solution.py:15
  350.0 12.0 collective-permute-start.28
  355.6 95.3 %collective-permute-start.25 = (bf16[1024,2048]{1,0:T(8,128)(2,1)}, bf16[1024,2048]{1,0:T(8,128)(2,1)}, u32[]{:S(2)}, u32[]{:S(2)}) collective-permute-start(bf16[1024,2048]{1,0:T(8,128)(2,1)} %maximum_select_fusion.3), channel_id=1, source_target_pairs={{0,2},{1,3},{2,0},{3,1},{4,6},{5,7},{6,4},{7,5},{8,10},{9,11},{10,... | collective-permute-start | bytes 12582920 | tf_op jit(solution)/shard_map/ppermute | solution.py:15
  362.2 88.6 %copy-start.37 = (bf16[256,2048]{1,0:T(8,128)(2,1)}, bf16[256,2048]{1,0:T(8,128)(2,1)S(1)}, u32[]{:S(2)}) copy-start(bf16[256,2048]{1,0:T(8,128)(2,1)S(1)} %maximum_select_fusion.34) | copy-start | bytes 3145732
  362.2 36.0 %collective-permute-start.29 = (bf16[256,2048]{1,0:T(8,128)(2,1)S(1)}, bf16[256,2048]{1,0:T(8,128)(2,1)}, u32[]{:S(2)}, u32[]{:S(2)}) collective-permute-start(bf16[256,2048]{1,0:T(8,128)(2,1)S(1)} %maximum_select_fusion.34), channel_id=1, source_target_pairs={{0,8},{1,9},{2,10},{3,11},{4,12},{5,13},{6,14},{7,15},{8,0},{9,1},... | collective-permute-start | bytes 3145736 | tf_op jit(solution)/shard_map/ppermute | solution.py:15
  492.5 48.0 %collective-permute-start.26 = (bf16[256,2048]{1,0:T(8,128)(2,1)S(1)}, bf16[256,2048]{1,0:T(8,128)(2,1)}, u32[]{:S(2)}, u32[]{:S(2)}) collective-permute-start(bf16[256,2048]{1,0:T(8,128)(2,1)S(1)} %select_convert_fusion.13), channel_id=1, source_target_pairs={{0,8},{1,9},{2,10},{3,11},{4,12},{5,13},{6,14},{7,15},{8,0},{9,1},... | collective-permute-start | bytes 3145736 | tf_op jit(solution)/shard_map/ppermute | solution.py:15
  493.9 41.7 %collective-permute-start.30 = (bf16[256,2048]{1,0:T(8,128)(2,1)S(1)}, bf16[256,2048]{1,0:T(8,128)(2,1)}, u32[]{:S(2)}, u32[]{:S(2)}) collective-permute-start(bf16[256,2048]{1,0:T(8,128)(2,1)S(1)} %select_convert_fusion.12), channel_id=1, source_target_pairs={{0,8},{1,9},{2,10},{3,11},{4,12},{5,13},{6,14},{7,15},{8,0},{9,1},... | collective-permute-start | bytes 3145736 | tf_op jit(solution)/shard_map/ppermute | solution.py:15
  538.7 9.6 collective-permute-start.31
  542.4 17.4 %collective-permute-start.27 = (bf16[128,2048]{1,0:T(8,128)(2,1)S(1)}, bf16[128,2048]{1,0:T(8,128)(2,1)S(1)}, u32[]{:S(2)}, u32[]{:S(2)}) collective-permute-start(bf16[128,2048]{1,0:T(8,128)(2,1)S(1)} %select_convert_fusion.22), channel_id=1, source_target_pairs={{0,4},{1,5},{2,6},{3,7},{4,0},{5,1},{6,2},{7,3},{8,12},{9,13},{10,... | collective-permute-start | bytes 1572872 | tf_op jit(solution)/shard_map/ppermute | solution.py:15
  561.6 9.5 collective-permute-start.32
  565.7 281.5 %collective-permute-start.48 = (bf16[2048,1024]{1,0:T(8,128)(2,1)}, bf16[2048,1024]{1,0:T(8,128)(2,1)}, u32[]{:S(2)}, u32[]{:S(2)}) collective-permute-start(bf16[2048,1024]{1,0:T(8,128)(2,1)} %select_convert_fusion.1), channel_id=1, source_target_pairs={{0,2},{1,3},{2,0},{3,1},{4,6},{5,7},{6,4},{7,5},{8,10},{9,11},{10,... | collective-permute-start | bytes 12582920 | tf_op jit(solution)/shard_map/ppermute | solution.py:15
  571.4 18.4 %collective-permute-start.33 = (bf16[256,2048]{1,0:T(8,128)(2,1)S(1)}, bf16[256,2048]{1,0:T(8,128)(2,1)S(1)}, u32[]{:S(2)}, u32[]{:S(2)}) collective-permute-start(bf16[256,2048]{1,0:T(8,128)(2,1)S(1)} %maximum_select_fusion.35), channel_id=1, source_target_pairs={{0,8},{1,9},{2,10},{3,11},{4,12},{5,13},{6,14},{7,15},{8,0},{9,1},... | collective-permute-start | bytes 3145736 | tf_op jit(solution)/shard_map/ppermute | solution.py:15
  588.4 448.6 %collective-permute-start.50 = (bf16[1024,2048]{1,0:T(8,128)(2,1)}, bf16[1024,2048]{1,0:T(8,128)(2,1)}, u32[]{:S(2)}, u32[]{:S(2)}) collective-permute-start(bf16[1024,2048]{1,0:T(8,128)(2,1)} %select_convert_fusion), channel_id=1, source_target_pairs={{0,2},{1,3},{2,0},{3,1},{4,6},{5,7},{6,4},{7,5},{8,10},{9,11},{10,... | collective-permute-start | bytes 12582920 | tf_op jit(solution)/shard_map/ppermute | solution.py:15
  642.1 130.6 %collective-permute-start.46 = (bf16[256,2048]{1,0:T(8,128)(2,1)S(1)}, bf16[256,2048]{1,0:T(8,128)(2,1)S(1)}, u32[]{:S(2)}, u32[]{:S(2)}) collective-permute-start(bf16[256,2048]{1,0:T(8,128)(2,1)S(1)} %select_convert_fusion.6), channel_id=1, source_target_pairs={{0,2},{1,3},{2,0},{3,1},{4,6},{5,7},{6,4},{7,5},{8,10},{9,11},{10,... | collective-permute-start | bytes 3145736 | tf_op jit(solution)/shard_map/ppermute | solution.py:15
  643.4 151.7 %collective-permute-start.36 = (bf16[1024,512]{0,1:T(8,128)(2,1)S(1)}, bf16[1024,512]{0,1:T(8,128)(2,1)S(1)}, u32[]{:S(2)}, u32[]{:S(2)}) collective-permute-start(bf16[1024,512]{0,1:T(8,128)(2,1)S(1)} %bitcast.146), channel_id=1, source_target_pairs={{0,2},{1,3},{2,0},{3,1},{4,6},{5,7},{6,4},{7,5},{8,10},{9,11},{10,... | collective-permute-start | bytes 3145736 | tf_op jit(solution)/shard_map/ppermute | solution.py:15
  644.1 173.5 %collective-permute-start.34 = (bf16[1024,512]{0,1:T(8,128)(2,1)S(1)}, bf16[1024,512]{0,1:T(8,128)(2,1)S(1)}, u32[]{:S(2)}, u32[]{:S(2)}) collective-permute-start(bf16[1024,512]{0,1:T(8,128)(2,1)S(1)} %bitcast.145), channel_id=1, source_target_pairs={{0,2},{1,3},{2,0},{3,1},{4,6},{5,7},{6,4},{7,5},{8,10},{9,11},{10,... | collective-permute-start | bytes 3145736 | tf_op jit(solution)/shard_map/ppermute | solution.py:15
  772.7 67.4 %collective-permute-start.40 = (bf16[2048,256]{1,0:T(8,128)(2,1)S(1)}, bf16[2048,256]{1,0:T(8,128)(2,1)S(1)}, u32[]{:S(2)}, u32[]{:S(2)}) collective-permute-start(bf16[2048,256]{1,0:T(8,128)(2,1)S(1)} %select_convert_fusion.9), channel_id=1, source_target_pairs={{0,2},{1,3},{2,0},{3,1},{4,6},{5,7},{6,4},{7,5},{8,10},{9,11},{10,... | collective-permute-start | bytes 3145736 | tf_op jit(solution)/shard_map/ppermute | solution.py:15
  795.1 59.6 %collective-permute-start.47 = (bf16[128,2048]{1,0:T(8,128)(2,1)S(1)}, bf16[128,2048]{1,0:T(8,128)(2,1)}, u32[]{:S(2)}, u32[]{:S(2)}) collective-permute-start(bf16[128,2048]{1,0:T(8,128)(2,1)S(1)} %select_convert_fusion.15), channel_id=1, source_target_pairs={{0,1},{1,0},{2,3},{3,2},{4,5},{5,4},{6,7},{7,6},{8,9},{9,8},{10,11... | collective-permute-start | bytes 1572872 | tf_op jit(solution)/shard_map/ppermute | solution.py:15
  817.6 39.2 %collective-permute-start.37 = (bf16[512,512]{0,1:T(8,128)(2,1)}, bf16[512,512]{0,1:T(8,128)(2,1)}, u32[]{:S(2)}, u32[]{:S(2)}) collective-permute-start(bf16[512,512]{0,1:T(8,128)(2,1)} %select_convert_fusion.19), channel_id=1, source_target_pairs={{0,1},{1,0},{2,3},{3,2},{4,5},{5,4},{6,7},{7,6},{8,9},{9,8},{10,11... | collective-permute-start | bytes 1572872 | tf_op jit(solution)/shard_map/ppermute | solution.py:15
  840.1 28.1 %collective-permute-start.35 = (bf16[512,512]{0,1:T(8,128)(2,1)}, bf16[512,512]{0,1:T(8,128)(2,1)}, u32[]{:S(2)}, u32[]{:S(2)}) collective-permute-start(bf16[512,512]{0,1:T(8,128)(2,1)} %select_convert_fusion.20), channel_id=1, source_target_pairs={{0,1},{1,0},{2,3},{3,2},{4,5},{5,4},{6,7},{7,6},{8,9},{9,8},{10,11... | collective-permute-start | bytes 1572872 | tf_op jit(solution)/shard_map/ppermute | solution.py:15
  847.2 40.4 %collective-permute-start.41 = (bf16[2048,128]{1,0:T(8,128)(2,1)S(1)}, bf16[2048,128]{1,0:T(8,128)(2,1)}, u32[]{:S(2)}, u32[]{:S(2)}) collective-permute-start(bf16[2048,128]{1,0:T(8,128)(2,1)S(1)} %select_convert_fusion.18), channel_id=1, source_target_pairs={{0,1},{1,0},{2,3},{3,2},{4,5},{5,4},{6,7},{7,6},{8,9},{9,8},{10,11... | collective-permute-start | bytes 1572872 | tf_op jit(solution)/shard_map/ppermute | solution.py:15
  856.8 199.2 %reduce-scatter.7.cloned.1.call-start = ((), (), s32[]{:S(2)}) async-start(), calls=%async_computation.8 | async-start | bytes 589824 | tf_op jit(solution)/shard_map/reduce_scatter | solution.py:326
  865.8 25.3 %collective-permute-start.44 = (bf16[2048,256]{1,0:T(8,128)(2,1)}, bf16[2048,256]{1,0:T(8,128)(2,1)}, u32[]{:S(2)}, u32[]{:S(2)}) collective-permute-start(bf16[2048,256]{1,0:T(8,128)(2,1)} %select_convert_fusion.7), channel_id=1, source_target_pairs={{0,2},{1,3},{2,0},{3,1},{4,6},{5,7},{6,4},{7,5},{8,10},{9,11},{10,... | collective-permute-start | bytes 3145736 | tf_op jit(solution)/shard_map/ppermute | solution.py:15
  878.0 73.0 %collective-permute-start.38 = (bf16[256,6144]{1,0:T(8,128)(2,1)}, bf16[256,6144]{1,0:T(8,128)(2,1)}, u32[]{:S(2)}, u32[]{:S(2)}) collective-permute-start(bf16[256,6144]{1,0:T(8,128)(2,1)} %select_convert_fusion.2), channel_id=1, source_target_pairs={{0,8},{1,9},{2,10},{3,11},{4,12},{5,13},{6,14},{7,15},{8,0},{9,1},... | collective-permute-start | bytes 9437192 | tf_op jit(solution)/shard_map/ppermute | solution.py:15
  886.7 26.9 %collective-permute-start.42 = (bf16[2048,256]{1,0:T(8,128)(2,1)S(1)}, bf16[2048,256]{1,0:T(8,128)(2,1)}, u32[]{:S(2)}, u32[]{:S(2)}) collective-permute-start(bf16[2048,256]{1,0:T(8,128)(2,1)S(1)} %select_convert_fusion.8), channel_id=1, source_target_pairs={{0,2},{1,3},{2,0},{3,1},{4,6},{5,7},{6,4},{7,5},{8,10},{9,11},{10,... | collective-permute-start | bytes 3145736 | tf_op jit(solution)/shard_map/ppermute | solution.py:15
  889.8 185.0 %reduce-scatter.11.cloned.1.call-start = ((), (), s32[]{:S(2)}) async-start(), calls=%async_computation.10 | async-start | bytes 589824 | tf_op jit(solution)/shard_map/reduce_scatter | solution.py:332
  894.1 70.4 %collective-permute-start.45 = (bf16[2048,128]{1,0:T(8,128)(2,1)S(1)}, bf16[2048,128]{1,0:T(8,128)(2,1)S(1)}, u32[]{:S(2)}, u32[]{:S(2)}) collective-permute-start(bf16[2048,128]{1,0:T(8,128)(2,1)S(1)} %select_convert_fusion.16), channel_id=1, source_target_pairs={{0,1},{1,0},{2,3},{3,2},{4,5},{5,4},{6,7},{7,6},{8,9},{9,8},{10,11... | collective-permute-start | bytes 1572872 | tf_op jit(solution)/shard_map/ppermute | solution.py:15
  915.3 56.3 %collective-permute-start.43 = (bf16[2048,128]{1,0:T(8,128)(2,1)S(1)}, bf16[2048,128]{1,0:T(8,128)(2,1)}, u32[]{:S(2)}, u32[]{:S(2)}) collective-permute-start(bf16[2048,128]{1,0:T(8,128)(2,1)S(1)} %select_convert_fusion.17), channel_id=1, source_target_pairs={{0,1},{1,0},{2,3},{3,2},{4,5},{5,4},{6,7},{7,6},{8,9},{9,8},{10,11... | collective-permute-start | bytes 1572872 | tf_op jit(solution)/shard_map/ppermute | solution.py:15
  962.5 36.7 %collective-permute-start.39 = (bf16[128,6144]{1,0:T(8,128)(2,1)}, bf16[128,6144]{1,0:T(8,128)(2,1)}, u32[]{:S(2)}, u32[]{:S(2)}) collective-permute-start(bf16[128,6144]{1,0:T(8,128)(2,1)} %select_convert_fusion.5), channel_id=1, source_target_pairs={{0,4},{1,5},{2,6},{3,7},{4,0},{5,1},{6,2},{7,3},{8,12},{9,13},{10,... | collective-permute-start | bytes 4718600 | tf_op jit(solution)/shard_map/ppermute | solution.py:15
  965.5 183.4 %reduce-scatter.9.cloned.1.call-start = ((), (), s32[]{:S(2)}) async-start(), calls=%async_computation.9 | async-start | bytes 589824 | tf_op jit(solution)/shard_map/reduce_scatter | solution.py:329
  970.7 59.5 %collective-permute-start.49 = (bf16[2048,512]{1,0:T(8,128)(2,1)}, bf16[2048,512]{1,0:T(8,128)(2,1)}, u32[]{:S(2)}, u32[]{:S(2)}) collective-permute-start(bf16[2048,512]{1,0:T(8,128)(2,1)} %select_convert_fusion.4), channel_id=1, source_target_pairs={{0,1},{1,0},{2,3},{3,2},{4,5},{5,4},{6,7},{7,6},{8,9},{9,8},{10,11... | collective-permute-start | bytes 6291464 | tf_op jit(solution)/shard_map/ppermute | solution.py:15
  973.8 181.2 %all-reduce.10.cloned.1.call-start = ((), (), s32[]{:S(2)}) async-start(), calls=%async_computation.6 | async-start | bytes 1179648 | tf_op jit(solution)/shard_map/psum | solution.py:310
  1030.2 251.4 %reduce-scatter.15.cloned.1.call-start = ((), (), s32[]{:S(2)}) async-start(), calls=%async_computation.12 | async-start | bytes 2359296 | tf_op jit(solution)/shard_map/reduce_scatter | solution.py:338
  1036.9 267.7 %reduce-scatter.17.cloned.1.call-start = ((), (), s32[]{:S(2)}) async-start(), calls=%async_computation.13 | async-start | bytes 2359296 | tf_op jit(solution)/shard_map/reduce_scatter | solution.py:341
  1046.1 5.8 collective-permute-start.51
  1054.4 98.5 %copy-start.73 = (f32[128]{0:T(128)S(1)}, f32[128]{0:T(128)}, u32[]{:S(2)}) copy-start(f32[128]{0:T(128)} %copy-done.72) | copy-start | bytes 1540
  1054.4 334.0 %all-reduce.12.cloned.1.call-start = ((), (), s32[]{:S(2)}) async-start(), calls=%async_computation.7 | async-start | bytes 1179648 | tf_op jit(solution)/shard_map/psum | solution.py:309
  1076.2 78.8 %copy-start.27 = (f32[128,4,17]{2,1,0:T(4,128)S(1)}, f32[128,4,17]{2,1,0:T(4,128)}, u32[]{:S(2)}) copy-start(f32[128,4,17]{2,1,0:T(4,128)} %copy-done.26) | copy-start | bytes 104452
  (97 other events, 1412.5 us)
Sparse Core Ops, SparseCore 0:
  856.9 71.2 reduce-scatter.12
  932.7 69.2 reduce-scatter.6
  1005.5 69.2 reduce-scatter.10
  1079.1 69.7 reduce-scatter.8
  1152.5 74.3 reduce-scatter.14
  1230.5 74.0 reduce-scatter.16
  1307.2 81.1 all-reduce.11
Sparse Core Ops, SparseCore 1:
  1030.2 118.8 all-reduce.9
